TPU v7x, 32 devices: a whole 2x2x4 slice. The times are simulated.
32 devices in a mesh: seq: 8 (over y, x, core), col: 4 (over z).
Axes of the slice: x: 2, y: 2, z: 4, core: 2. Of those that a mesh axis runs over, the one named last changes fastest.
Arguments:
- inputs: bfloat16 [16384, 2048], P(('seq', 'col'))
- norm_gain: float32 [2048], replicated, may hold values from 0.5 to 1.5
- norm_bias: float32 [2048], replicated, may hold values from -3 to 3
- weight: bfloat16 [2048, 6144], P(None, 'col'), may hold values from -0.125 to 0.125
- forget_peep: float32 [2048], P('col'), may hold values from -1 to 1
- reset_peep: float32 [2048], P('col'), may hold values from -1.5 to 1.5
- forget_bias: float32 [2048], P('col')
- reset_bias: float32 [2048], P('col'), may hold values from -4 to 4
- seq_lengths: int32 [4], replicated, may hold values from 1 to 15701, as said below
- out_grad: bfloat16 [16384, 2048], P('seq', 'col'), may hold values from -6 to 6
Outputs:
- output: bfloat16 [16384, 2048], P('seq', 'col')
- input_grad: float32 [16384, 2048], P(('seq', 'col'))
- weight_grad: float32 [2048, 6144], P(None, 'col')
- gain_grad: float32 [2048], replicated
- bias_grad: float32 [2048], replicated
- forget_peep_grad: float32 [2048], P('col')
- reset_peep_grad: float32 [2048], P('col')
- forget_bias_grad: float32 [2048], P('col')
- reset_bias_grad: float32 [2048], P('col')
Inputs may be any that keep to these rules, and one draw needn't show every extreme that they name: `seq_lengths`: the 4 sequences fill all 16384 tokens end to end. One of them, at a place drawn from the seed, begins within the first 2048 tokens and ends within the last 2048; each other one is shorter than 682.
All inputs are finite; a program needn't handle non-finite values.
Results may differ from a plain program's by a relative error of at most 0.014.
Values may be sent and summed in bfloat16 or wider, within the bound.
No kernel may reach another device: no remote copies, remote signals or barrier semaphores. Data moves between devices by JAX's collectives and lax.ppermute only.
A program may use at most 192 MiB of HBM per device.

v0:
```python
import jax
import jax.numpy as jnp
from jax import lax
from jax.sharding import PartitionSpec as P

EPSILON = 1e-05


def from_behind(value, axis, steps):
    count = lax.axis_size(axis)
    leading, last = (max(0, -steps), min(count, count - steps))
    return lax.ppermute(value, axis, [(source, source + steps) for source in range(leading, last)])


def compose(earlier, latter):
    return (earlier[0] * latter[0], latter[0] * earlier[1] + latter[1])


def layer_norm(row_values, norm_gain, norm_bias):
    average = jnp.mean(row_values, axis=-1, keepdims=True)
    centred = row_values - average
    inv_scale = lax.rsqrt(jnp.mean(centred * centred, axis=-1, keepdims=True) + EPSILON)
    return centred * inv_scale * norm_gain + norm_bias


def per_device(
    inputs,
    norm_gain,
    norm_bias,
    weight,
    forget_peep,
    reset_peep,
    forget_bias,
    reset_bias,
    seq_lengths,
    out_grad,
):
    local_rows = inputs.shape[0]
    width = inputs.shape[1]
    groups = lax.axis_size("col")
    channels = width // groups
    row_values = inputs.astype(jnp.float32)
    normed, norm_pullback = jax.vjp(layer_norm, row_values, norm_gain, norm_bias)
    normed_low = normed.astype(jnp.bfloat16)
    full_weight = lax.all_gather(weight, "col", axis=1, tiled=True)
    mixed = jnp.dot(normed_low, full_weight, preferred_element_type=jnp.float32)
    mixed_low = mixed.astype(jnp.bfloat16).reshape(local_rows, 3, groups, channels)
    streams, highway = (
        lax.all_to_all(mixed_low, "col", split_axis=2, concat_axis=0, tiled=True),
        lax.all_to_all(
            inputs.reshape(local_rows, 1, groups, channels),
            "col",
            split_axis=2,
            concat_axis=0,
            tiled=True,
        ),
    )
    block_rows = streams.shape[0]
    candidate = streams[:, 0, 0].astype(jnp.float32)
    forget_pre = streams[:, 1, 0].astype(jnp.float32)
    reset_pre = streams[:, 2, 0].astype(jnp.float32)
    skip_values = highway[:, 0, 0].astype(jnp.float32)
    positions = lax.axis_index("seq") * block_rows + jnp.arange(block_rows, dtype=jnp.int32)
    bounds = jnp.cumsum(seq_lengths) - seq_lengths
    starts = jnp.any(positions[:, None] == bounds[None, :], axis=1)
    kept_mask = 1.0 - starts.astype(jnp.float32)[:, None]
    forget = jax.nn.sigmoid(forget_pre + forget_peep * candidate + forget_bias)
    decay = forget * kept_mask
    inject = (1.0 - forget) * candidate
    run_decay, run_state = lax.associative_scan(compose, (decay, inject), axis=0)
    block_map = (run_decay[-1], run_state[-1])

    def relay(turn_index, carried):
        return from_behind(block_map[0] * carried + block_map[1], "seq", 1)

    carry_in = lax.fori_loop(
        0, lax.axis_size("seq") - 1, relay, jnp.zeros((channels,), jnp.float32)
    )
    cell_state = run_decay * carry_in + run_state
    previous = jnp.concatenate([carry_in[None, :], cell_state[:-1]], axis=0) * kept_mask
    reset = jax.nn.sigmoid(reset_pre + reset_peep * previous + reset_bias)
    output = (reset * cell_state + (1.0 - reset) * skip_values).astype(jnp.bfloat16)
    grad_out = out_grad.astype(jnp.float32)
    reset_z = grad_out * (cell_state - skip_values) * reset * (1.0 - reset)
    direct = grad_out * reset
    skip_grad = (grad_out * (1.0 - reset)).astype(jnp.bfloat16)
    prev_grad = reset_z * reset_peep
    back_decay = kept_mask * forget
    back_inject = kept_mask * (forget * direct + prev_grad)
    flipped = lax.associative_scan(compose, (back_decay[::-1], back_inject[::-1]), axis=0)
    run_back_decay = flipped[0][::-1]
    run_back = flipped[1][::-1]
    back_map = (run_back_decay[0], run_back[0])

    def relay_back(turn_index, carried):
        return from_behind(back_map[0] * carried + back_map[1], "seq", -1)

    back_in = lax.fori_loop(
        0, lax.axis_size("seq") - 1, relay_back, jnp.zeros((channels,), jnp.float32)
    )
    back_values = run_back_decay * back_in + run_back
    cell_grad = direct + jnp.concatenate([back_values[1:], back_in[None, :]], axis=0)
    forget_z = cell_grad * (previous - candidate) * forget * (1.0 - forget)
    candidate_grad = cell_grad * (1.0 - forget) + forget_z * forget_peep
    gate_sums = jnp.stack(
        [
            jnp.sum(forget_z * candidate, axis=0),
            jnp.sum(reset_z * previous, axis=0),
            jnp.sum(forget_z, axis=0),
            jnp.sum(reset_z, axis=0),
        ]
    )
    stream_grads = jnp.stack([candidate_grad, forget_z, reset_z], axis=1).astype(jnp.bfloat16)
    back_streams, back_skip = (
        lax.all_to_all(stream_grads[:, :, None, :], "col", split_axis=0, concat_axis=2, tiled=True),
        lax.all_to_all(skip_grad[:, None, None, :], "col", split_axis=0, concat_axis=2, tiled=True),
    )
    mixed_grad = back_streams.reshape(local_rows, 3 * width)
    normed_grad = lax.dot_general(
        mixed_grad, full_weight, (((1,), (1,)), ((), ())), preferred_element_type=jnp.float32
    )
    row_grad, gain_part, bias_part = norm_pullback(normed_grad)
    input_grad = row_grad + back_skip.reshape(local_rows, width).astype(jnp.float32)
    seq_count = lax.axis_size("seq")
    piece_rows = 3 * width // (groups * seq_count)
    ordered = (
        mixed_grad.reshape(local_rows, groups, seq_count, piece_rows)
        .transpose(0, 2, 1, 3)
        .reshape(local_rows, 3 * width)
    )
    partial_grad = lax.psum_scatter(
        lax.dot_general(
            ordered, normed_low, (((0,), (0,)), ((), ())), preferred_element_type=jnp.float32
        ).astype(jnp.bfloat16),
        "seq",
        scatter_dimension=0,
        tiled=True,
    ).astype(jnp.float32)
    partial_grad = lax.psum_scatter(
        partial_grad.astype(jnp.bfloat16), "col", scatter_dimension=0, tiled=True
    ).astype(jnp.float32)
    block_grad = lax.all_gather(partial_grad, "seq", axis=0, tiled=True)
    weight_grad = block_grad.T
    group_offset = lax.axis_index("col") * channels
    spread = lax.dynamic_update_slice_in_dim(
        jnp.zeros((4, width), jnp.float32), gate_sums, group_offset, 1
    )
    gain_grad, bias_grad, gate_total = lax.psum((gain_part, bias_part, spread), ("seq", "col"))
    gate_block = lax.dynamic_slice_in_dim(gate_total, group_offset, channels, 1)
    return (
        output,
        input_grad,
        weight_grad,
        gain_grad,
        bias_grad,
        gate_block[0],
        gate_block[1],
        gate_block[2],
        gate_block[3],
    )


def solution(mesh):
    placed = (
        P(("seq", "col"), None),
        P(),
        P(),
        P(None, "col"),
        P("col"),
        P("col"),
        P("col"),
        P("col"),
        P(),
        P("seq", "col"),
    )
    return jax.shard_map(
        per_device,
        mesh=mesh,
        in_specs=placed,
        out_specs=(
            P("seq", "col"),
            P(("seq", "col"), None),
            P(None, "col"),
            P(),
            P(),
            P("col"),
            P("col"),
            P("col"),
            P("col"),
        ),
        check_vma=False,
    )
```

profile of v0, /device:TPU:12, one launch (start us, length us, event | category | flops | bytes accessed | tf_op | source)
XLA Modules:
  0.0 1998.7 jit_solution(8521408123395106153)
XLA Ops:
  10.4 422.8 %all-gather.3.cloned.1.call-done = bf16[2048,6144]{1,0:T(8,128)(2,1)} async-done(((bf16[2048,1536]{1,0:T(8,128)(2,1)}), bf16[2048,6144]{1,0:T(8,128)(2,1)}) %all-gather.3.cloned.1.call-update) | async-done | bytes 25165840 | tf_op jit(solution)/shard_map/all_gather | solution.py:45
  433.2 19.9 convolution_convert_fusion.1
  453.1 13.4 reshape.171
  488.7 128.4 %all-to-all-done = bf16[512,3,4,512]{3,0,1,2:T(8,128)(2,1)} async-done(((bf16[512,3,4,512]{3,0,1,2:T(8,128)(2,1)}), bf16[512,3,4,512]{3,0,1,2:T(8,128)(2,1)}, u32[]{:S(2)}, u32[]{:S(2)}) %all-to-all-start) | async-done | bytes 6291488 | tf_op jit(solution)/shard_map/all_to_all | solution.py:49
  644.7 11.2 slice.701
  656.7 11.3 slice.804
  668.0 11.2 slice.755
  679.2 11.2 slice.754
  690.4 16.7 slice.809
  765.3 11.4 slice.751
  776.6 11.2 slice.858
  835.2 16.7 pad.311
  855.9 16.5 pad.289
  900.8 40.6 %while.20 = (s32[]{:T(128)}, f32[512]{0:T(512)S(1)}, f32[512]{0:T(512)S(1)}, f32[512]{0:T(512)S(1)}, s32[]{:T(128)}) while((s32[]{:T(128)}, f32[512]{0:T(512)S(1)}, f32[512]{0:T(512)S(1)}, f32[512]{0:T(512)S(1)}, s32[]{:T(128)}) %tuple.128), condition=%wide.region_5.6_spmd, body=%wide.region_4.5_spmd.sunk | while | flops 1026 | bytes 16485 | solution.py:76
  965.1 11.2 slice.914
  986.3 11.2 slice.862
  997.5 16.6 slice.863
  1091.0 17.2 slice.915
  1164.1 16.7 pad.354
  1198.6 16.7 pad.332
  1231.4 32.6 %rev.9 = f32[2048,512]{1,0:T(8,128)} reverse(f32[2048,512]{1,0:T(8,128)} %add.642), dimensions={0} | reverse | bytes 8388608 | tf_op jit(solution)/shard_map/rev | solution.py:92
  1264.1 32.8 %rev.8 = f32[2048,512]{1,0:T(8,128)} reverse(f32[2048,512]{1,0:T(8,128)} %add.609), dimensions={0} | reverse | bytes 8388608 | tf_op jit(solution)/shard_map/rev | solution.py:91
  1296.9 38.0 %while.21 = (s32[]{:T(128)}, f32[512]{0:T(512)S(1)}, f32[512]{0:T(512)S(1)}, f32[512]{0:T(512)S(1)}, s32[]{:T(128)}) while((s32[]{:T(128)}, f32[512]{0:T(512)S(1)}, f32[512]{0:T(512)S(1)}, f32[512]{0:T(512)S(1)}, s32[]{:T(128)}) %tuple.126), condition=%wide.region_7.8_spmd, body=%wide.region_6.7_spmd.sunk | while | flops 1026 | bytes 16485 | solution.py:98
  1363.0 25.0 %copy.78 = bf16[2048,3,1,512]{3,1,2,0:T(4,128)(2,1)S(1)} copy(bf16[2048,3,1,512]{3,0,2,1:T(8,128)(2,1)S(1)} %pad_maximum_fusion) | data formatting | bytes 12582912 | tf_op jit(solution)/shard_map/stack | solution.py:113
  1388.0 183.7 %all_to_all.51 = bf16[2048,3,1,512]{3,1,2,0:T(4,128)(2,1)S(1)} all-to-all(bf16[2048,3,1,512]{3,1,2,0:T(4,128)(2,1)S(1)} %copy.78), channel_id=1, replica_groups=mesh['seq'=8,'col'=4] {'col'}, dimensions={0} | all-to-all | bytes 12582912 | tf_op jit(solution)/shard_map/all_to_all | solution.py:115
  1591.0 19.8 convolution_convert_fusion
  1610.9 157.6 %reduce-scatter.3.cloned.1.call-done = bf16[768,2048]{1,0:T(8,128)(2,1)} async-done(((bf16[6144,2048]{1,0:T(8,128)(2,1)}), bf16[768,2048]{1,0:T(8,128)(2,1)}) %reduce-scatter.3.cloned.1.call-update) | async-done | bytes 3145744 | tf_op jit(solution)/shard_map/reduce_scatter | solution.py:131
  1768.6 62.2 %reduce-scatter.5.cloned.1.call-done = bf16[192,2048]{1,0:T(8,128)(2,1)} async-done(((bf16[768,2048]{1,0:T(8,128)(2,1)}), bf16[192,2048]{1,0:T(8,128)(2,1)}) %reduce-scatter.5.cloned.1.call-update) | async-done | bytes 786448 | tf_op jit(solution)/shard_map/reduce_scatter | solution.py:139
  1848.7 44.9 %all-to-all-done.3 = bf16[4,2,131072]{2,1,0:T(2,128)(2,1)} async-done(((bf16[4,2,131072]{2,1,0:T(2,128)(2,1)}), bf16[4,2,131072]{2,1,0:T(2,128)(2,1)}, u32[]{:S(2)}, u32[]{:S(2)}) %all-to-all-start.3) | async-done | bytes 2097184 | tf_op jit(solution)/shard_map/all_to_all | solution.py:116
  1907.7 17.3 fusion.63
  1929.1 43.8 %all-reduce.88 = (f32[2048]{0:T(1024)}, f32[2048]{0:T(1024)}, f32[4,2048]{1,0:T(4,128)S(1)}) all-reduce(f32[2048]{0:T(1024)S(1)} %get-tuple-element.118, f32[2048]{0:T(1024)S(1)} %get-tuple-element.124, f32[4,2048]{1,0:T(4,128)S(1)} %maximum_dynamic-update-slice_fusion), channel_id=1, replica_groups=mesh['seq'=8,'col'=4] {'seq','col'}, use_global_device_ids=true, to_apply=%region_13.14 | all-reduce | flops 12288 | bytes 98304 | tf_op jit(solution)/shard_map/psum | solution.py:148
  1979.2 12.6 copy.85
  (562 shorter events, 558.5 us)
Async XLA Ops:
  7.2 426.0 %copy-start.36 = (f32[2048]{0:T(1024)S(1)}, f32[2048]{0:T(1024)}, u32[]{:S(2)}) copy-start(f32[2048]{0:T(1024)} %param.15) | copy-start | bytes 24580
  7.2 426.0 %copy-start.50 = (f32[2048]{0:T(1024)S(1)}, f32[2048]{0:T(1024)}, u32[]{:S(2)}) copy-start(f32[2048]{0:T(1024)} %param.16) | copy-start | bytes 24580
  7.2 426.0 %all-gather.3.cloned.1.call-start = ((), (), s32[]{:S(2)}) async-start(), calls=%async_computation.6 | async-start | bytes 31457280 | tf_op jit(solution)/shard_map/all_gather | solution.py:45
  9.1 443.9 %copy-start.40 = (f32[512]{0:T(512)}, f32[512]{0:T(512)S(1)}, u32[]{:S(2)}) copy-start(f32[512]{0:T(512)S(1)} %broadcast_multiply_fusion.1) | copy-start | bytes 6148
  10.4 442.7 %copy-start.42 = (f32[512]{0:T(512)}, f32[512]{0:T(512)S(1)}, u32[]{:S(2)}) copy-start(f32[512]{0:T(512)S(1)} %fusion.59) | copy-start | bytes 6148
  473.3 143.8 %all-to-all-start = ((bf16[512,3,4,512]{3,0,1,2:T(8,128)(2,1)}), bf16[512,3,4,512]{3,0,1,2:T(8,128)(2,1)}, u32[]{:S(2)}, u32[]{:S(2)}) async-start(bf16[512,3,4,512]{3,0,1,2:T(8,128)(2,1)} %copy.74), calls=%async_computation | async-start | bytes 12582912 | tf_op jit(solution)/shard_map/all_to_all | solution.py:49
  617.1 334.4 %all-to-all-start.1 = ((bf16[512,1,4,512]{3,0,1,2:T(8,128)(2,1)}), bf16[512,1,4,512]{3,0,1,2:T(8,128)(2,1)}, u32[]{:S(2)}, u32[]{:S(2)}) async-start(bf16[512,1,4,512]{3,0,1,2:T(8,128)(2,1)} %copy.77), calls=%async_computation.1 | async-start | bytes 4194304 | tf_op jit(solution)/shard_map/all_to_all | solution.py:50
  624.9 1143.7 %reduce-scatter.3.cloned.1.call-start = ((), (), s32[]{:S(2)}) async-start(), calls=%async_computation.7 | async-start | bytes 28311552 | tf_op jit(solution)/shard_map/reduce_scatter | solution.py:131
  722.8 19.0 copy-start.13
  805.6 21.4 %copy-start.24 = (f32[512,512]{1,0:T(8,128)S(1)}, f32[512,512]{1,0:T(8,128)}, u32[]{:S(2)}) copy-start(f32[512,512]{1,0:T(8,128)} %add.588) | copy-start | bytes 3145732
  900.8 5.8 collective-permute-start
  906.6 5.8 collective-permute-start
  912.4 5.8 collective-permute-start
  918.2 5.8 collective-permute-start
  924.0 5.8 collective-permute-start
  929.8 5.8 collective-permute-start
  935.6 5.8 collective-permute-start
  941.4 17.7 slice-start
  1126.2 21.5 %copy-start.25 = (f32[512,512]{1,0:T(8,128)S(1)}, f32[512,512]{1,0:T(8,128)}, u32[]{:S(2)}) copy-start(f32[512,512]{1,0:T(8,128)} %add.607) | copy-start | bytes 3145732
  1164.1 16.7 copy-start.19
  1264.1 75.5 %slice-start.2 = ((s8[6291456]{0:T(1024)(128)(4,1)}), s8[2097152]{0:T(1024)(128)(4,1)S(1)}, s32[]{:S(2)}) async-start(s8[6291456]{0:T(1024)(128)(4,1)} %bitcast.119), calls=%async_computation.12 | async-start | bytes 4194304
  1296.9 3.2 collective-permute-start.1
  1300.1 5.8 collective-permute-start.1
  1305.9 5.8 collective-permute-start.1
  1311.7 5.8 collective-permute-start.1
  1317.5 5.8 collective-permute-start.1
  1323.3 5.8 collective-permute-start.1
  1329.1 5.8 collective-permute-start.1
  1610.9 219.9 %reduce-scatter.5.cloned.1.call-start = ((), (), s32[]{:S(2)}) async-start(), calls=%async_computation.8 | async-start | bytes 3932160 | tf_op jit(solution)/shard_map/reduce_scatter | solution.py:139
  1768.6 210.6 %all-gather.5.cloned.1.call-start = ((), (), s32[]{:S(2)}) async-start(), calls=%async_computation.9 | async-start | bytes 14155776 | tf_op jit(solution)/shard_map/all_gather | solution.py:142
  1842.9 50.7 %all-to-all-start.3 = ((bf16[4,2,131072]{2,1,0:T(2,128)(2,1)}), bf16[4,2,131072]{2,1,0:T(2,128)(2,1)}, u32[]{:S(2)}, u32[]{:S(2)}) async-start(bf16[4,2,131072]{2,1,0:T(2,128)(2,1)} %reshape.184), calls=%async_computation.3 | async-start | bytes 4194304 | tf_op jit(solution)/shard_map/all_to_all | solution.py:116
  1907.7 17.3 copy-start.45
  (48 other events, 225.5 us)
Sparse Core Ops, SparseCore 0:
  9.6 423.5 all-gather.2
  1611.0 157.5 reduce-scatter.2
  1770.9 59.8 reduce-scatter.4
  1833.4 72.0 all-gather.4
where the time goes:
time: 2020 us; the launch traced here: 2000 us
  waiting for transfers between devices  853 us (42%)
  local copies, waits for them, and re-layouts  633 us (31%)
  blocking collectives  227 us (11%)
  other arithmetic  147 us (7%)
  starting transfers between devices  64.5 us (3%)
  matrix products  57 us (3%)
    all_gather x1, waiting for transfers between devices, per_device(): full_weight = lax.all_gather(weight, 'col', axis=1, tiled=True)  423 us
    all_to_all x1, blocking collectives, per_device(): lax.all_to_all(stream_grads[:, :, None, :], 'col', split_axis=0, concat_a...  184 us
    slice x80, local copies, waits for them, and re-layouts, per_device(): lax.associative_scan(compose, (back_decay[::-1], back_inject[::-1]), axis=0)  170 us
    reduce_scatter x1, waiting for transfers between devices, per_device(): lax.psum_scatter(lax.dot_general(ordered, normed_low, (((0,), (0,)), ((),...  158 us
    all_to_all x1, waiting for transfers between devices, per_device(): lax.all_to_all(mixed_low, 'col', split_axis=2, concat_axis=0, tiled=True)  128 us
    slice x75, local copies, waits for them, and re-layouts, per_device(): lax.associative_scan(compose, (decay, inject), axis=0)  105 us
    pad x40, local copies, waits for them, and re-layouts, per_device(): lax.associative_scan(compose, (back_decay[::-1], back_inject[::-1]), axis=0)  85.3 us
    pad x40, local copies, waits for them, and re-layouts, per_device(): lax.associative_scan(compose, (decay, inject), axis=0)  84.9 us
  transfers between devices with their start and end apart: 21, of which 19 were waited for; matrix products, arithmetic and copies ran while one was open for 17% of the time, Pallas kernels for 0%

commit v1 on v0

v1 whole, which is shorter than its diff:
```python
import functools

import jax
import jax.numpy as jnp
import numpy as np
from jax import lax
from jax.experimental import pallas as pl
from jax.experimental.pallas import tpu as pltpu
from jax.sharding import PartitionSpec as P

EPSILON = 1e-05
F32 = jnp.float32
BF16 = jnp.bfloat16
LANES = 128
SUB = 8
VMEM_LIMIT = 56 * 1024 * 1024


def bits_of(count):
    return [1 << b for b in range(count.bit_length() - 1)]


def colour(edges, count):
    degree = max([sum(e[0] == n for e in edges) for n in range(count)] + [sum(e[1] == n for e in edges) for n in range(count)])
    out = [[None] * degree for _ in range(count)]
    into = [[None] * degree for _ in range(count)]
    taken = {}
    for at, edge in enumerate(edges):
        src, dst = edge[0], edge[1]
        first = next(c for c in range(degree) if out[src][c] is None)
        second = next(c for c in range(degree) if into[dst][c] is None)
        if first != second:
            path, node, at_dst, look = [], dst, True, first
            while True:
                found = (into if at_dst else out)[node][look]
                if found is None:
                    break
                path.append(found)
                node = edges[found][0] if at_dst else edges[found][1]
                at_dst = not at_dst
                look = second if look == first else first
            for found in path:
                old = taken[found]
                out[edges[found][0]][old] = None
                into[edges[found][1]][old] = None
            for found in path:
                new = second if taken[found] == first else first
                taken[found] = new
                out[edges[found][0]][new] = found
                into[edges[found][1]][new] = found
        taken[at] = first
        out[src][first] = at
        into[dst][first] = at
    rounds = [[] for _ in range(degree)]
    for at, edge in enumerate(edges):
        rounds[taken[at]].append(edge)
    return rounds


def routes(groups, streams):
    low = groups // 2
    plans = []
    for core in range(2):
        local, edges = [], []
        for dst in range(groups):
            for stream in streams:
                block = stream * groups + dst % low + low * core
                src, at = block // 3, block % 3
                (local if src == dst else edges).append((src, dst, stream, at))
        plans.append((local, colour(edges, groups)))
    count = max(len(rounds) for _, rounds in plans)
    return [(local, rounds + [[]] * (count - len(rounds))) for local, rounds in plans], count


def row_order(rows):
    seg = rows // SUB
    matrix = np.zeros((rows, rows), np.float32)
    for i in range(seg):
        for j in range(SUB):
            matrix[i * SUB + j, j * seg + i] = 1.0
    return matrix


def gate(value):
    small = jnp.exp(-jnp.abs(value))
    minor = small / (1.0 + small)
    major = 1.0 - minor
    up = value >= 0.0
    return jnp.where(up, major, minor), jnp.where(up, minor, major)


def kept_of(base, step, seg, bounds, channels):
    at = lax.broadcasted_iota(jnp.int32, (SUB, LANES), 0) * seg + (base + step)
    starts = at == bounds[0]
    for bound in bounds[1:]:
        starts = starts | (at == bound)
    kept = jnp.where(starts, 0.0, 1.0)
    return jnp.concatenate([kept] * (channels // LANES), axis=1)


class Info:
    def __init__(self):
        self.spots = {}
        self.columns = []

    def put(self, name, values):
        self.spots[name] = len(self.columns)
        self.columns += list(np.asarray(values, np.int32))

    def __getattr__(self, name):
        return self.spots[name]

    def table(self):
        return np.stack(self.columns, axis=1)


def bounds_of(lengths):
    starts = [0]
    for n in range(lengths.shape[0] - 1):
        starts.append(starts[-1] + lengths[n])
    return starts


def cut_kernel(count, copies, s, block_ref, *out_refs):
    part = block_ref.shape[0]
    for n in range(count):

        @pl.when(pl.program_id(0) == n)
        def _():
            for copy in range(copies):
                out_refs[n][copy * part : (copy + 1) * part] = block_ref[...]


def pick_kernel(name, info, sources, s, *refs):
    came, outs = refs[:sources], refs[sources:]
    outs = list(outs) if len(outs) > 1 else [outs[0].at[n] for n in range(outs[0].shape[0])]
    for n, out in enumerate(outs):
        for r in range(sources):

            @pl.when(s[getattr(info, name) + n] == r)
            def _():
                out[...] = came[r][...]


def norm_rows(x_ref, gain, bias, normed_ref, hat_ref, inv_ref):
    block = 32
    for r in range(x_ref.shape[0] // block):
        at = slice(r * block, (r + 1) * block)
        x = x_ref[at].astype(F32)
        average = jnp.mean(x, axis=1, keepdims=True)
        centred = x - average
        inv = lax.rsqrt(jnp.mean(centred * centred, axis=1, keepdims=True) + EPSILON)
        hat = centred * inv
        normed_ref[0, at] = (hat * gain + bias).astype(BF16)
        hat_ref[0, at] = hat.astype(BF16)
        inv_ref[0, at] = jnp.broadcast_to(inv, (block, LANES))


def group_columns(info, s, channels):
    return pl.ds(pl.multiple_of(s[info.g] * channels, channels), channels)


def norm_kernel(info, s, x_ref, gain_ref, bias_ref, *refs):
    normed_ref, hx_ref, hat_ref, inv_ref = refs[-4:]
    norm_rows(x_ref, gain_ref[...], bias_ref[...], normed_ref, hat_ref, inv_ref)
    hx_ref[0] = x_ref[:, group_columns(info, s, hx_ref.shape[2])]


def segment_maps(base, seg, lengths, mixed_ref, fp, fb):
    channels = mixed_ref.shape[3]
    run_decay = jnp.ones((SUB, channels), F32)
    run_state = jnp.zeros((SUB, channels), F32)
    bounds = bounds_of(lengths)
    for i in range(mixed_ref.shape[2] // SUB):
        at = slice(i * SUB, (i + 1) * SUB)
        candidate = mixed_ref[0, 0, at].astype(F32)
        forget, rest = gate(mixed_ref[0, 1, at].astype(F32) + fp * candidate + fb)
        decay = forget * kept_of(base, i, seg, bounds, channels)
        run_state = decay * run_state + rest * candidate
        run_decay = decay * run_decay
    return run_decay, run_state


def mix_kernel(info, low, planes, seg, here, away, split, s, lengths, normed_ref, fp_ref, fb_ref, *refs):
    count = here + (planes + 1 if split else planes)
    pieces = refs[:count]
    mixed_ref, map_ref, full_ref, w_ref, in_sem, out_sem = refs[count:]
    part = w_ref.shape[1] // planes
    parts = [(d, 0, part) for d in range(planes)]
    if split:
        parts = parts[:3] + [(3, 0, part // 2), (3, part // 2, part // 2)]
    step = pl.program_id(0)

    def copies(slot):
        stream = s[info.slot_stream + slot]
        if slot < here:
            return [pltpu.make_async_copy(pieces[slot], w_ref.at[stream], in_sem.at[slot])]
        found = []
        for n, (d, start, size) in enumerate(parts):
            rows = pl.ds(pl.multiple_of((d ^ s[info.p]) * part + start, size), size)
            piece = pieces[here + n].at[slot - here]
            spot = here + (slot - here) * len(parts) + n
            found.append(pltpu.make_async_copy(piece, w_ref.at[stream, rows, :], in_sem.at[spot]))
        return found

    @pl.when(step == 0)
    def _():
        for slot in range(here + away):

            @pl.when(s[info.slot_stream + slot] >= 0)
            def _():
                for copy in copies(slot):
                    copy.start()

        for slot in range(here + away):

            @pl.when(s[info.slot_stream + slot] >= 0)
            def _():
                for copy in copies(slot):
                    copy.wait()

        pltpu.make_async_copy(w_ref, full_ref, out_sem).start()

    for stream in range(3):
        mixed_ref[0, stream] = jnp.dot(normed_ref[0], w_ref[stream], preferred_element_type=F32).astype(BF16)
    decay, state = segment_maps(s[info.base + step * low], seg, lengths, mixed_ref, fp_ref[...], fb_ref[...])
    map_ref[0, 0] = decay
    map_ref[0, 1] = state

    @pl.when(step == pl.num_programs(0) - 1)
    def _():
        pltpu.make_async_copy(w_ref, full_ref, out_sem).wait()


def mix_far_kernel(info, low, seg, order, tile, s, lengths, w_ref, gain_ref, bias_ref, fp_ref, fb_ref, near_ref, *refs):
    count = len(order)
    pieces = refs[: 2 * count]
    normed_ref, hx_ref, hat_ref, inv_ref, mixed_ref, map_ref, run_ref, x_ref, sem = refs[2 * count + 5 :]
    channels = w_ref.shape[2]
    step = pl.program_id(0)

    def copies(n):
        return [
            pltpu.make_async_copy(pieces[2 * n], x_ref.at[n, pl.ds(0, tile), :], sem.at[2 * n]),
            pltpu.make_async_copy(pieces[2 * n + 1], x_ref.at[n, pl.ds(tile, x_ref.shape[1] - tile), :], sem.at[2 * n + 1]),
        ]

    @pl.when(step == 0)
    def _():
        for n in range(count):
            for copy in copies(n):
                copy.start()
        for dk in range(2):
            map_ref[dk * low] = near_ref[dk * low]

    for n in range(count):

        @pl.when(step == n)
        def _():
            for copy in copies(n):
                copy.wait()

    mine = x_ref.at[step]
    norm_rows(mine, gain_ref[...], bias_ref[...], normed_ref, hat_ref, inv_ref)
    hx_ref[0] = mine[:, group_columns(info, s, channels)]
    for stream in range(3):
        mixed_ref[0, stream] = jnp.dot(normed_ref[0], w_ref[stream], preferred_element_type=F32).astype(BF16)
    chunk = far_chunk(low, step)
    decay, state = segment_maps(s[info.base + chunk], seg, lengths, mixed_ref, fp_ref[...], fb_ref[...])
    map_ref[chunk, 0] = decay
    map_ref[chunk, 1] = state

    @pl.when(step == count - 1)
    def _():
        rows = []
        for dk in range(2):
            decay = jnp.ones((1, channels), F32)
            state = jnp.zeros((1, channels), F32)
            for zl in range(low):
                c = dk * low + (zl ^ s[info.zlo])
                for j in range(SUB):
                    d, b = map_ref[c, 0, j : j + 1, :], map_ref[c, 1, j : j + 1, :]
                    state = d * state + b
                    decay = d * decay
            rows += [decay, state]
        run_ref[...] = jnp.concatenate(rows + [jnp.zeros((4, channels), F32)], axis=0)


def far_chunk(low, n):
    return n // (low - 1) * low + 1 + n % (low - 1)


def gathered_maps(info, planes, s, refs, into):
    for d in range(planes):
        plane = d ^ s[info.p]
        into[s[info.zhi] * planes + plane] = refs[d][...]
        into[(1 - s[info.zhi]) * planes + plane] = refs[planes][d]


def state_kernel(info, low, planes, seg, s, lengths, *refs):
    gathered_refs = refs[: planes + 1]
    (
        map_ref, mixed_ref, hx_ref, og_ref, og_far_ref, order_ref, back_order_ref, fp_ref, rp_ref, fb_ref, rb_ref,
        out_ref, out_far_ref, prev_ref, direct_ref, rz_ref, rzb_ref, skip_ref, binj_ref, sums_ref, runb_ref,
        cell_ref, prod_ref, kept_out_ref, gathered_ref,
    ) = refs[planes + 1 :]
    chunks, channels = map_ref.shape[0], map_ref.shape[3]
    step = pl.program_id(0)
    last = pl.num_programs(0) - 1
    k, zlo = s[info.k], s[info.zlo]

    @pl.when(step == 0)
    def _():
        gathered_maps(info, planes, s, gathered_refs, gathered_ref)
        carry = jnp.zeros((1, channels), F32)
        own = [carry, carry]
        for plane in range(planes):
            for core in range(2):
                for zh in range(2):
                    e = zh * planes + plane
                    mine = (plane == s[info.p]) & (zh == s[info.zhi])
                    own[core] = jnp.where(mine, carry, own[core])
                    decay = jnp.where(k == core, gathered_ref[e, 0:1, :], gathered_ref[e, 2:3, :])
                    state = jnp.where(k == core, gathered_ref[e, 1:2, :], gathered_ref[e, 3:4, :])
                    carry = decay * carry + state
        for dk in range(2):
            carry = jnp.where(k == 0, own[dk], own[1 - dk])
            for zl in range(low):
                c = dk * low + (zl ^ zlo)
                for j in range(SUB):
                    cell_ref[c, j : j + 1, :] = carry
                    carry = map_ref[c, 0, j : j + 1, :] * carry + map_ref[c, 1, j : j + 1, :]
        prod_ref[...] = jnp.ones_like(prod_ref)
        binj_ref[...] = jnp.zeros_like(binj_ref)
        sums_ref[...] = jnp.zeros_like(sums_ref)

    rows = hx_ref.shape[1]
    steps = rows // SUB
    bounds = bounds_of(lengths)
    fp, rp, fb, rb = fp_ref[...], rp_ref[...], fb_ref[...], rb_ref[...]
    rz_sum, peep_sum = sums_ref[0], sums_ref[1]
    for c in range(chunks):
        dk, dz = c // low, c % low
        grad = jnp.dot(order_ref[...], (og_ref, og_far_ref)[dk][dz ^ zlo], preferred_element_type=F32)
        base = s[info.base + c]
        cell, prod, binj = cell_ref[c], prod_ref[c], binj_ref[c]
        for i in range(steps):
            at = slice(i * SUB, (i + 1) * SUB)
            candidate = mixed_ref[c, 0, at].astype(F32)
            forget, rest = gate(mixed_ref[c, 1, at].astype(F32) + fp * candidate + fb)
            kept = kept_of(base, step * steps + i, seg, bounds, channels)
            previous = kept * cell
            decay = forget * kept
            cell = forget * previous + rest * candidate
            reset, skip = gate(mixed_ref[c, 2, at].astype(F32) + rp * previous + rb)
            x = hx_ref[c, at].astype(F32)
            g = grad[at]
            kept_out_ref[c, pl.ds(pl.multiple_of(step * rows + i * SUB, SUB), SUB), :] = reset * cell + skip * x
            direct = g * reset
            g_skip = g * skip
            rz = direct * skip * (cell - x)
            prev_ref[c, at] = previous
            direct_ref[c, at] = direct
            rz_ref[c, at] = rz
            rzb_ref[c, at] = rz.astype(BF16)
            skip_ref[c, at] = g_skip.astype(BF16)
            binj = binj + prod * (decay * direct + kept * (rz * rp))
            prod = prod * decay
            rz_sum = rz_sum + rz
            peep_sum = peep_sum + rz * previous
        cell_ref[c] = cell
        prod_ref[c] = prod
        binj_ref[c] = binj
    sums_ref[0] = rz_sum
    sums_ref[1] = peep_sum

    @pl.when(step == last)
    def _():
        for c in range(chunks):
            dk, dz = c // low, c % low
            (out_ref, out_far_ref)[dk][dz ^ zlo] = jnp.dot(
                back_order_ref[...], kept_out_ref[c].astype(BF16), preferred_element_type=F32
            ).astype(BF16)
        runs = []
        for dk in range(2):
            acc = jnp.zeros((1, channels), F32)
            for zl in reversed(range(low)):
                c = dk * low + (zl ^ zlo)
                for j in reversed(range(SUB)):
                    acc = binj_ref[c, j : j + 1, :] + map_ref[c, 0, j : j + 1, :] * acc
            runs.append(acc)
        runb_ref[...] = jnp.concatenate(runs + [jnp.zeros((6, channels), F32)], axis=0)


def back_kernel(info, low, planes, seg, s, lengths, *refs):
    gathered_refs, back_refs = refs[: planes + 1], refs[planes + 1 : 2 * planes + 2]
    (
        map_ref, binj_ref, mixed_ref, prev_ref, direct_ref, rz_ref, fp_ref, rp_ref, fb_ref,
        grad_c_ref, grad_f_ref, sums_ref,
        carry_ref, gathered_ref, back_ref,
    ) = refs[2 * planes + 2 :]
    chunks, channels = map_ref.shape[0], map_ref.shape[3]
    step = pl.program_id(0)
    count = pl.num_programs(0)
    k, zlo = s[info.k], s[info.zlo]

    @pl.when(step == 0)
    def _():
        gathered_maps(info, planes, s, gathered_refs, gathered_ref)
        gathered_maps(info, planes, s, back_refs, back_ref)
        carry = jnp.zeros((1, channels), F32)
        own = [carry, carry]
        for plane in reversed(range(planes)):
            for core in (1, 0):
                for zh in (1, 0):
                    e = zh * planes + plane
                    mine = (plane == s[info.p]) & (zh == s[info.zhi])
                    own[core] = jnp.where(mine, carry, own[core])
                    decay = jnp.where(k == core, gathered_ref[e, 0:1, :], gathered_ref[e, 2:3, :])
                    inject = jnp.where(k == core, back_ref[e, 0:1, :], back_ref[e, 1:2, :])
                    carry = decay * carry + inject
        for dk in range(2):
            carry = jnp.where(k == 0, own[dk], own[1 - dk])
            for zl in reversed(range(low)):
                c = dk * low + (zl ^ zlo)
                for j in reversed(range(SUB)):
                    carry_ref[c, j : j + 1, :] = carry
                    carry = map_ref[c, 0, j : j + 1, :] * carry + binj_ref[c, j : j + 1, :]
        sums_ref[...] = jnp.zeros_like(sums_ref)

    rows = prev_ref.shape[1]
    steps = rows // SUB
    bounds = bounds_of(lengths)
    fp, rp, fb = fp_ref[...], rp_ref[...], fb_ref[...]
    fz_sum, peep_sum = sums_ref[0], sums_ref[1]
    for c in range(chunks):
        base = s[info.base + c]
        back = carry_ref[c]
        for i in reversed(range(steps)):
            at = slice(i * SUB, (i + 1) * SUB)
            candidate = mixed_ref[c, 0, at].astype(F32)
            forget, rest = gate(mixed_ref[c, 1, at].astype(F32) + fp * candidate + fb)
            kept = kept_of(base, (count - 1 - step) * steps + i, seg, bounds, channels)
            cell_grad = direct_ref[c, at] + back
            back = kept * (forget * cell_grad + rz_ref[c, at] * rp)
            held = cell_grad * rest
            forget_z = held * forget * (prev_ref[c, at] - candidate)
            grad_c_ref[c, at] = (held + forget_z * fp).astype(BF16)
            grad_f_ref[c, at] = forget_z.astype(BF16)
            fz_sum = fz_sum + forget_z
            peep_sum = peep_sum + forget_z * candidate
        carry_ref[c] = back
    sums_ref[0] = fz_sum
    sums_ref[1] = peep_sum


def input_kernel(info, joined, s, grad_c_ref, grad_f_ref, rzb_ref, w_ref, gain_ref, hat_ref, inv_ref, skip_ref, *refs):
    v_ref, s_ref, gb_ref, grad_ref, first_ref, second_ref = refs[1:] if joined else refs
    tile = pl.program_id(0)
    nt = (((1,), (1,)), ((), ()))
    grad = lax.dot_general(grad_c_ref[0], w_ref[0], nt, preferred_element_type=F32)
    grad = grad + lax.dot_general(grad_f_ref[0], w_ref[1], nt, preferred_element_type=F32)
    grad_ref[...] = grad + lax.dot_general(rzb_ref[0], w_ref[2], nt, preferred_element_type=F32)

    @pl.when(tile == 0)
    def _():
        first_ref[...] = jnp.zeros_like(first_ref)
        second_ref[...] = jnp.zeros_like(second_ref)

    rows, width = grad_ref.shape
    flag = jnp.where(s[info.g] == tile, 1.0, 0.0)
    gain = gain_ref[...]
    block = 32
    gain_sum = jnp.zeros((SUB, width), F32)
    bias_sum = jnp.zeros((SUB, width), F32)
    for r in range(rows // block):
        at = slice(r * block, (r + 1) * block)
        value = grad_ref[at]
        inv = jnp.concatenate([inv_ref[0, at]] * (width // LANES), axis=1)
        hat = hat_ref[0, at].astype(F32)
        scaled = value * gain
        product = scaled * hat
        first, second = first_ref[at], second_ref[at]
        for lane in range(width // LANES):
            first = first + scaled[:, lane * LANES : (lane + 1) * LANES]
            second = second + product[:, lane * LANES : (lane + 1) * LANES]
        first_ref[at] = first
        second_ref[at] = second
        matched = value * hat
        for i in range(block // SUB):
            gain_sum = gain_sum + matched[i * SUB : (i + 1) * SUB]
            bias_sum = bias_sum + value[i * SUB : (i + 1) * SUB]
        out = scaled * inv + skip_ref[0, at].astype(F32) * flag
        if joined:
            out = out + refs[0][at].astype(F32)
        v_ref[at] = out.astype(BF16)
    gb_ref[0] = gain_sum
    gb_ref[1] = bias_sum

    @pl.when(tile == pl.num_programs(0) - 1)
    def _():
        lane = lax.broadcasted_iota(jnp.int32, (rows, LANES), 1)
        first = jnp.sum(first_ref[...], axis=1, keepdims=True)
        second = jnp.sum(second_ref[...], axis=1, keepdims=True)
        s_ref[...] = jnp.where(lane == 0, first, jnp.where(lane == 1, second, 0.0)).T[:SUB]


def last_kernel(count, x_ref, order_ref, *refs):
    parts, (s_ref, out_ref) = refs[:count], refs[count:]
    width = x_ref.shape[1]
    x = x_ref[...].astype(F32)
    average = jnp.mean(x, axis=1, keepdims=True)
    centred = x - average
    inv = lax.rsqrt(jnp.mean(centred * centred, axis=1, keepdims=True) + EPSILON)
    order = order_ref[...]
    value = jnp.dot(order, parts[0][...], preferred_element_type=F32)
    for part in parts[1:]:
        value = value + jnp.dot(order, part[...], preferred_element_type=F32)
    sums = lax.dot_general(
        order.astype(F32), s_ref[...], (((1,), (1,)), ((), ())),
        precision=lax.Precision.HIGHEST, preferred_element_type=F32,
    )
    first = sums[:, 0:1] * (1.0 / width)
    second = sums[:, 1:2] * (1.0 / width)
    out_ref[...] = value - inv * (first + centred * inv * second)


def weight_grad_kernel(order, s, normed_ref, grads_ref, *out_refs):
    tn = (((0,), (0,)), ((), ()))
    total = lax.dot_general(normed_ref[0], grads_ref[0], tn, preferred_element_type=F32)
    for c in range(1, normed_ref.shape[0]):
        total = total + lax.dot_general(normed_ref[c], grads_ref[c], tn, preferred_element_type=F32)
    low = total.astype(BF16)
    half = low.shape[0] // 2
    for at, places in enumerate(order):

        @pl.when(pl.program_id(0) == at)
        def _():
            for ref, place, rows in places:
                out_refs[ref][place] = (low, low[:half], low[half:])[rows]


def owned_kernel(info, count, s, *refs):
    came, outs, total_ref, slot_ref, sem = refs[:count], refs[count : count + 2], *refs[count + 2 :]
    total_ref[...] = jnp.zeros_like(total_ref)
    for wait in (False, True):
        for n in range(count):

            @pl.when(s[info.owned + n] >= 0)
            def _():
                copy = pltpu.make_async_copy(came[n], slot_ref.at[n], sem.at[n])
                if not wait:
                    copy.start()
                else:
                    copy.wait()
                    total_ref[s[info.owned + n]] += slot_ref[n].astype(F32)

    half = total_ref.shape[1] // 2
    for n, out in enumerate(outs):
        core = s[info.k] if n == 0 else 1 - s[info.k]
        rows = pl.ds(pl.multiple_of(core * half, half), half)
        for block in range(3):
            out[block] = total_ref[block, rows, :].astype(BF16)


def spread_kernel(count, steps, s, *refs):
    pieces, out_ref = refs[:count], refs[-1]
    rows, channels = out_ref.shape[0], pieces[0].shape[2]
    for n, (piece, start) in enumerate(steps):

        @pl.when(pl.program_id(0) == n)
        def _():
            for block in range(3):
                values = pieces[piece][block, start : start + rows]
                out_ref[:, block * channels : (block + 1) * channels] = values.astype(F32)


def cost(flops, moved, exps=0):
    return pl.CostEstimate(flops=int(flops), bytes_accessed=int(moved), transcendentals=int(exps))


def per_device(
    inputs, norm_gain, norm_bias, weight, forget_peep, reset_peep, forget_bias, reset_bias, seq_lengths, out_grad
):
    rows, width = inputs.shape
    seqs, groups = lax.axis_size("seq"), lax.axis_size("col")
    planes, low = seqs // 2, groups // 2
    channels = width // groups
    chunks = groups
    seg = rows // SUB
    part = width // planes
    half, quarter = part // 2, part // 4
    seq, z = lax.axis_index("seq"), lax.axis_index("col")
    k, zhi = seq % 2, z // low
    params = functools.partial(pltpu.CompilerParams, vmem_limit_bytes=VMEM_LIMIT)
    others = range(1, planes)
    short = planes == 4
    anywhere = pl.BlockSpec(memory_space=pl.ANY)
    full = lambda shape: pl.BlockSpec(shape, lambda *_: (0,) * len(shape))
    shape_of = jax.ShapeDtypeStruct

    def move(value, to):
        pairs = []
        for a in range(seqs):
            for b in range(groups):
                target = to(a // 2, a % 2, b)
                if target is not None:
                    pairs.append((a * groups + b, (target[0] * 2 + target[1]) * groups + target[2]))
        return lax.ppermute(value, ("seq", "col"), pairs)

    def cross_core(value):
        return move(value, lambda p, k, z: (p, 1 - k, z))

    def cross_low(value, dz):
        return move(value, lambda p, k, z: (p, k, z ^ dz))

    def cross_high(value):
        return move(value, lambda p, k, z: (p, k, (z + low) % groups))

    def cross_plane(value, dp):
        return move(value, lambda p, k, z: (p ^ dp, k, z))

    def after(values, *first):
        return lax.optimization_barrier((values, first))[0]

    def gather_maps(value):
        near = [value] + [cross_plane(value, d) for d in others]
        return near + [cross_high(jnp.stack(near))]

    def add_up(values):
        total = values[0].astype(F32)
        for value in values[1:]:
            total = total + value.astype(F32)
        return total.astype(BF16)

    device = np.arange(seqs * groups)
    dev_p, dev_k, dev_z = device // groups // 2, device // groups % 2, device % groups
    dev_zhi, dev_zlo = dev_z // low, dev_z % low
    info = Info()
    for name, value in (("p", dev_p), ("k", dev_k), ("zhi", dev_zhi), ("zlo", dev_zlo), ("g", dev_zlo + low * dev_k)):
        info.put(name, [value])
    info.put(
        "base",
        [((2 * dev_p + (dev_k ^ (c // low))) * groups + dev_zhi * low + (dev_zlo ^ (c % low))) * rows for c in range(chunks)],
    )
    at_dev = lambda table: np.asarray(table)[:, dev_k, dev_z]
    plans, rounds = routes(groups, range(3))
    here = max(sum(dst == n for _, dst, _, _ in local) for local, _ in plans for n in range(groups))
    away = 0
    slot_stream = np.full((6, 2, groups), -1, np.int32)
    slot_round = np.full((3, 2, groups), -1, np.int32)
    local_block = np.zeros((3, 2, groups), np.int32)
    sends_block = np.zeros((rounds, 2, groups), np.int32)
    for core, (local, plan) in enumerate(plans):
        for n in range(groups):
            for at, edge in enumerate(edge for edge in local if edge[1] == n):
                slot_stream[at, core, n] = edge[2]
                local_block[at, core, n] = edge[3]
            found = [(r, e[2]) for r, edges in enumerate(plan) for e in edges if e[1] == n]
            for at, (r, stream) in enumerate(found):
                slot_stream[here + at, core, n] = stream
                slot_round[at, core, n] = r
            away = max(away, len(found))
        for r, edges in enumerate(plan):
            for src, _, _, at in edges:
                sends_block[r, core, src] = at
    info.put("slot_stream", at_dev(slot_stream[: here + away]))
    info.put("slot_round", at_dev(slot_round[:away]))
    info.put("local_block", at_dev(local_block))
    info.put("sends_block", at_dev(sends_block))
    back_routes = [(streams, *routes(groups, streams)) for streams in ([0, 2], [1])]
    owned, back_stream = [], []
    for streams, back_plans, count in back_routes:
        for r in range(count):
            takes = np.full((2, groups), -1, np.int32)
            source = np.zeros((2, groups), np.int32)
            for core, (_, plan) in enumerate(back_plans):
                for src, dst, stream, at in plan[r]:
                    takes[core, src] = at
                    source[core, dst] = streams.index(stream)
            owned.append(takes)
            back_stream.append(source)
        for stream in streams:
            takes = np.full((2, groups), -1, np.int32)
            for core, (local, _) in enumerate(back_plans):
                for src, _, found, at in local:
                    if found == stream:
                        takes[core, src] = at
            owned.append(takes)
    info.put("owned", at_dev(owned))
    info.put("back_stream", at_dev(back_stream[: back_routes[0][2]]))
    visits = [3, 1, 2, 0] if short else list(range(planes))
    info.put("visits", [dev_p ^ d for d in visits])
    whole_planes = range(3 if short else planes)
    split_planes = range(3, 4) if short else []
    for name, chosen in (("whole_rows", whole_planes), ("split_rows", split_planes)):
        found = [((dev_p ^ d) * 2 + (dev_k ^ dk)) * 2 + n for dk in range(2) for d in chosen for n in range(2)]
        info.put(name, np.asarray(found).reshape(-1, seqs * groups))
    scalars = lax.dynamic_index_in_dim(jnp.asarray(info.table()), seq * groups + z, 0, keepdims=False)

    order = jnp.asarray(row_order(rows), BF16)
    back_order = jnp.asarray(row_order(rows).T.copy(), BF16)

    def call(kernel, out_shape, in_specs, out_specs, grid=(1,), scratch=(), lengths=False, aliases=None, **rest):
        return pl.pallas_call(
            kernel,
            grid_spec=pltpu.PrefetchScalarGridSpec(
                num_scalar_prefetch=2 if lengths else 1,
                grid=grid,
                in_specs=in_specs,
                out_specs=out_specs,
                scratch_shapes=list(scratch),
            ),
            out_shape=out_shape,
            input_output_aliases=aliases or {},
            compiler_params=params(),
            **rest,
        )

    def cut(name, count, copies, first=()):
        source, row = after((weight, scalars), *first) if first else (weight, scalars)
        at = getattr(info, name)
        return call(
            functools.partial(cut_kernel, count, copies),
            [shape_of((copies * part, channels), BF16)] * count,
            [pl.BlockSpec((part, channels), lambda t, s: (s[info.p], s[at + t]))],
            [full((copies * part, channels))] * count,
            grid=(count,),
            cost_estimate=cost(0, 0),
            name="cut_weight",
        )(row, source)

    def round_to(plan, r):
        return {(core, e[0]): e[1] for core, (_, rounds_of) in enumerate(plan) for e in rounds_of[r]}

    blocks_out = cut("sends_block", rounds, 1)
    arrived = []
    for r in range(rounds):
        to = round_to(plans, r)
        arrived.append(move(blocks_out[r], lambda p, k, z: (p, k, to[(k, z)]) if (k, z) in to else None))
    permuted = jnp.dot(order, after(inputs, blocks_out), preferred_element_type=F32).astype(BF16)
    x_core = cross_core(permuted)
    plane_groups = [[2 * n + core for n in range(planes)] for core in range(2)]
    local_full = [
        lax.all_gather(value, "seq", axis_index_groups=plane_groups, tiled=True)
        for value in cut("local_block", here, 1, (permuted,))
    ]
    tile = 128 if rows % 128 == 0 else rows
    tiles = rows // tile
    early = [cross_low(permuted[:tile], dz) for dz in range(1, low)]

    gates = jnp.stack([forget_peep, reset_peep, forget_bias, reset_bias])
    gates_far = cross_high(after(gates, x_core))
    gates = jnp.where(zhi == k, gates, gates_far)
    fp, rp, fb, rb = (gates[n : n + 1] for n in range(4))

    half_rows = low * rows
    own_half = lax.dynamic_slice_in_dim(out_grad, zhi * half_rows, half_rows, 0)
    unit = half_rows // 32
    far_parts = []
    for start, size in ((0, 8), (8, 11), (19, 13)):
        far_parts.append(lax.dynamic_slice_in_dim(out_grad, (1 - zhi) * half_rows + start * unit, size * unit, 0))
    taken = call(
        functools.partial(pick_kernel, "slot_round", info, rounds),
        shape_of((away, part, channels), BF16),
        [full((part, channels))] * rounds,
        full((away, part, channels)),
        cost_estimate=cost(0, 3 * part * channels),
        name="pick_blocks",
    )(scalars, *arrived)
    taken, x_late, far_parts = after((taken, permuted[tile:], far_parts), local_full, x_core, early, gates)
    far_came = [cross_high(far_parts[0])]
    late = [cross_low(x_late, dz) for dz in range(1, low)]
    if short:
        near_one, near_two = cross_plane(taken, 1), cross_plane(taken, 2)
        taken_full = [taken, near_one, near_two]
        taken_ends = [cross_plane(near_one[:, :half], 2), cross_plane(near_two[:, half:], 1)]
    else:
        taken_full = [taken] + [cross_plane(taken, d) for d in others]
        taken_ends = []
    gain2, bias2 = norm_gain[None, :], norm_bias[None, :]

    row_shapes = (
        shape_of((chunks, rows, width), BF16),
        shape_of((chunks, rows, channels), BF16),
        shape_of((chunks, rows, width), BF16),
        shape_of((chunks, rows, LANES), F32),
    )
    mix_shapes = (shape_of((chunks, 3, rows, channels), BF16), shape_of((chunks, 2, SUB, channels), F32))
    wide = 256 if rows % 256 == 0 else rows

    def normalise(c, value, held):
        return call(
            functools.partial(norm_kernel, info),
            row_shapes,
            [pl.BlockSpec((wide, width), lambda t, s: (t, 0)), full((1, width)), full((1, width))]
            + [anywhere] * len(held),
            [
                pl.BlockSpec((1, wide, width), lambda t, s: (c, t, 0)),
                pl.BlockSpec((1, wide, channels), lambda t, s: (c, t, 0)),
                pl.BlockSpec((1, wide, width), lambda t, s: (c, t, 0)),
                pl.BlockSpec((1, wide, LANES), lambda t, s: (c, t, 0)),
            ],
            grid=(rows // wide,),
            aliases={4 + n: n for n in range(len(held))},
            cost_estimate=cost(12 * rows * width, 7 * rows * width),
            name="norm_chunk",
        )(scalars, value, gain2, bias2, *held)

    held = normalise(0, permuted, ())
    held = normalise(low, x_core, held)

    early, late, far_parts = after((early, late, far_parts), taken_full, taken_ends, held, far_came)
    cross = [(cross_core(a), cross_core(b)) for a, b in zip(early, late)]
    far_came.append(cross_high(far_parts[1]))
    mix_cost = cost(3 * chunks * rows * width * channels, 4 * chunks * rows * width + 12 * width * channels)
    mixed, maps, full_weight = call(
        functools.partial(mix_kernel, info, low, planes, seg, here, away, short),
        mix_shapes + (shape_of((3, width, channels), BF16),),
        [pl.BlockSpec((1, rows, width), lambda t, *_: (t * low, 0, 0)), full((1, channels)), full((1, channels))]
        + [anywhere] * (here + len(taken_full) + len(taken_ends)),
        [
            pl.BlockSpec((1, 3, rows, channels), lambda t, *_: (t * low, 0, 0, 0)),
            pl.BlockSpec((1, 2, SUB, channels), lambda t, *_: (t * low, 0, 0, 0)),
            anywhere,
        ],
        grid=(2,),
        scratch=[
            pltpu.VMEM((3, width, channels), BF16),
            pltpu.SemaphoreType.DMA((here + away * (planes + 1),)),
            pltpu.SemaphoreType.DMA,
        ],
        lengths=True,
        cost_estimate=mix_cost,
        name="mix_near",
    )(scalars, seq_lengths, held[0], fp, fb, *local_full, *taken_full, *taken_ends)

    mixed, far_parts = after((mixed, far_parts), far_came)
    far_came.append(cross_high(far_parts[2]))
    far_order = [far_chunk(low, n) for n in range(2 * (low - 1))]
    far_pieces = [(early[c % low - 1], late[c % low - 1]) if c < low else cross[c % low - 1] for c in far_order]
    far_at = lambda t: far_chunk(low, t)
    *held, mixed, maps, run_maps = call(
        functools.partial(mix_far_kernel, info, low, seg, far_order, tile),
        row_shapes + mix_shapes + (shape_of((SUB, channels), F32),),
        [full((3, width, channels)), full((1, width)), full((1, width)), full((1, channels)), full((1, channels))]
        + [full((chunks, 2, SUB, channels))]
        + [anywhere] * (2 * len(far_order))
        + [anywhere] * 5,
        [
            pl.BlockSpec((1, rows, width), lambda t, *_: (far_at(t), 0, 0)),
            pl.BlockSpec((1, rows, channels), lambda t, *_: (far_at(t), 0, 0)),
            pl.BlockSpec((1, rows, width), lambda t, *_: (far_at(t), 0, 0)),
            pl.BlockSpec((1, rows, LANES), lambda t, *_: (far_at(t), 0, 0)),
            pl.BlockSpec((1, 3, rows, channels), lambda t, *_: (far_at(t), 0, 0, 0)),
            full((chunks, 2, SUB, channels)),
            full((SUB, channels)),
        ],
        grid=(len(far_order),),
        scratch=[
            pltpu.VMEM((len(far_order), rows, width), BF16),
            pltpu.SemaphoreType.DMA((2 * len(far_order),)),
        ],
        lengths=True,
        aliases={8 + 2 * len(far_order) + n: n for n in range(5)},
        cost_estimate=mix_cost,
        name="mix_far",
    )(
        scalars, seq_lengths, full_weight, gain2, bias2, fp, fb, maps,
        *[piece for pair in far_pieces for piece in pair], *held, mixed,
    )
    normed, highway, hats, invs = held

    gathered = gather_maps(run_maps)
    far_half = jnp.concatenate(after(far_came, run_maps), axis=0)
    keep = jnp.where(zhi == k, own_half, far_half)
    give = cross_core(jnp.where(zhi == k, far_half, own_half))

    map_specs = [full((SUB, channels))] * planes + [full((planes, SUB, channels))]
    block = 64
    blocks = rows // block
    elements = chunks * rows * channels
    runs = (low, rows, channels)
    part_rows = (chunks, block, channels)
    at_block = lambda t, *_: (0, t, 0)
    state_out = call(
        functools.partial(state_kernel, info, low, planes, seg),
        (
            shape_of(runs, BF16),
            shape_of(runs, BF16),
            shape_of((chunks, rows, channels), F32),
            shape_of((chunks, rows, channels), F32),
            shape_of((chunks, rows, channels), F32),
            shape_of((chunks, rows, channels), BF16),
            shape_of((chunks, rows, channels), BF16),
            shape_of((chunks, SUB, channels), F32),
            shape_of((2, SUB, channels), F32),
            shape_of((SUB, channels), F32),
        ),
        map_specs
        + [
            full((chunks, 2, SUB, channels)),
            pl.BlockSpec((chunks, 3, block, channels), lambda t, *_: (0, 0, t, 0)),
            pl.BlockSpec(part_rows, at_block),
            full(runs),
            full(runs),
            pl.BlockSpec((block, rows), lambda t, *_: (t, 0)),
            full((rows, rows)),
        ]
        + [full((1, channels))] * 4,
        [full(runs), full(runs)]
        + [pl.BlockSpec(part_rows, at_block)] * 5
        + [full((chunks, SUB, channels)), full((2, SUB, channels)), full((SUB, channels))],
        grid=(blocks,),
        scratch=[
            pltpu.VMEM((chunks, SUB, channels), F32),
            pltpu.VMEM((chunks, SUB, channels), F32),
            pltpu.VMEM((chunks, rows, channels), F32),
            pltpu.VMEM((2 * planes, SUB, channels), F32),
        ],
        lengths=True,
        cost_estimate=cost(60 * elements, 30 * elements, 4 * elements),
        name="states",
    )(
        scalars, seq_lengths, *gathered, maps, mixed, highway, keep.reshape(runs), give.reshape(runs),
        order, back_order, fp, rp, fb, rb,
    )
    out_own, out_far, previous, direct, reset_z, reset_zb, skip, binj, reset_sums, run_back = state_out

    if short:
        places = [[(0, 1, 1), (1, 1, 2)], [(0, 0, 1), (3, 1, 2)], [(2, 1, 1), (1, 0, 2)], [(2, 0, 1), (3, 0, 2)]]
        part_shapes = [(2, half, channels)] * 4
    else:
        places = [[(d, 0, 0)] for d in visits]
        part_shapes = [(1, part, channels)] * planes

    def weight_part(source, name):
        return call(
            functools.partial(weight_grad_kernel, places),
            [shape_of(shape, BF16) for shape in part_shapes],
            [pl.BlockSpec((chunks, rows, part), lambda t, s: (0, 0, s[info.visits + t])), full((chunks, rows, channels))],
            [full(shape) for shape in part_shapes],
            grid=(planes,),
            cost_estimate=cost(2 * chunks * rows * width * channels, 4 * chunks * rows * width),
            name=name,
        )(scalars, normed, source)

    def first_sends(parts):
        if short:
            return [cross_plane(parts[0], 1), cross_plane(parts[1], 2)]
        return [cross_plane(parts[d], d) for d in others]

    def second_start(parts, came):
        if not short:
            return came
        return [add_up([parts[2][1], came[0][1]]), add_up([parts[3][1], came[1][1]])]

    def second_end(parts, came, over):
        if not short:
            return add_up([parts[0][0]] + [value[0] for value in came])
        first = add_up([parts[2][0], came[0][0], cross_plane(over[0], 2)])
        second = add_up([parts[3][0], came[1][0], cross_plane(over[1], 1)])
        return jnp.concatenate([first, second], axis=0)

    def second_sends(parts, came):
        return second_end(parts, came, second_start(parts, came))

    def to_owners(which, values):
        _, back_plans, count = back_routes[which]
        found = []
        for r in range(count):
            back = {(core, dst): src for (core, src), dst in round_to(back_plans, r).items()}
            found.append(move(values[r], lambda p, k, z: (p, k, back[(k, z)]) if (k, z) in back else None))
        return found

    near_back = [run_back] + [cross_plane(run_back, d) for d in others]
    reset_wg = weight_part(after(reset_zb, near_back), "weight_grad_reset")
    gathered_back = near_back + [after(cross_high(jnp.stack(near_back)), reset_wg)]
    got = after(cross_core(out_far), reset_wg)
    stay = jnp.where(k == zhi, out_own, got)
    leave = jnp.where(k == zhi, got, out_own).reshape(4, half_rows // 4, channels)
    binj, leave = after((binj, leave), reset_wg, leave, gathered_back)
    out_came = []

    def send_out(piece):
        out_came.append(cross_high(piece))

    send_out(leave[0])
    reset_came = first_sends(after(reset_wg, gathered_back))

    grad_c, grad_f, forget_sums = call(
        functools.partial(back_kernel, info, low, planes, seg),
        (
            shape_of((chunks, rows, channels), BF16),
            shape_of((chunks, rows, channels), BF16),
            shape_of((2, SUB, channels), F32),
        ),
        map_specs * 2
        + [
            full((chunks, 2, SUB, channels)),
            full((chunks, SUB, channels)),
            pl.BlockSpec((chunks, 2, block, channels), lambda t, *_: (0, 0, blocks - 1 - t, 0)),
        ]
        + [pl.BlockSpec(part_rows, lambda t, *_: (0, blocks - 1 - t, 0))] * 3
        + [full((1, channels))] * 3,
        [pl.BlockSpec(part_rows, lambda t, *_: (0, blocks - 1 - t, 0))] * 2 + [full((2, SUB, channels))],
        grid=(blocks,),
        scratch=[
            pltpu.VMEM((chunks, SUB, channels), F32),
            pltpu.VMEM((2 * planes, SUB, channels), F32),
            pltpu.VMEM((2 * planes, SUB, channels), F32),
        ],
        lengths=True,
        cost_estimate=cost(30 * elements, 20 * elements, 2 * elements),
        name="state_grads",
    )(scalars, seq_lengths, *gathered, *gathered_back, maps, binj, mixed, previous, direct, reset_z, fp, rp, fb)

    def chunk_grad(c, joined):
        extra = [pl.BlockSpec((rows, channels), lambda t, s: (0, t))] if joined is not None else []
        chunk_block = pl.BlockSpec((1, rows, channels), lambda t, s: (c, 0, 0))
        return call(
            functools.partial(input_kernel, info, joined is not None),
            (shape_of((rows, width), BF16), shape_of((SUB, rows), F32), shape_of((2, SUB, width), F32)),
            [
                chunk_block,
                chunk_block,
                chunk_block,
                pl.BlockSpec((3, channels, channels), lambda t, s: (0, t, 0)),
                pl.BlockSpec((1, channels), lambda t, s: (0, t)),
                pl.BlockSpec((1, rows, channels), lambda t, s: (c, 0, t)),
                pl.BlockSpec((1, rows, LANES), lambda t, s: (c, 0, 0)),
                chunk_block,
            ]
            + extra,
            [
                pl.BlockSpec((rows, channels), lambda t, s: (0, t)),
                full((SUB, rows)),
                pl.BlockSpec((2, SUB, channels), lambda t, s: (0, 0, t)),
            ],
            grid=(groups,),
            scratch=[
                pltpu.VMEM((rows, channels), F32),
                pltpu.VMEM((rows, LANES), F32),
                pltpu.VMEM((rows, LANES), F32),
            ],
            cost_estimate=cost(6 * rows * width * channels, 8 * rows * width + 6 * width * channels),
            name="chunk_grad",
        )(
            scalars, grad_c, grad_f, reset_zb, full_weight, gain2, hats, invs, skip,
            *([joined] if joined is not None else []),
        )

    norm_sums = []

    def grads_of(c, joined, *first):
        nonlocal grad_c
        grad_c = after(grad_c, *first)
        value, sums, gb = chunk_grad(c, joined)
        norm_sums.append(gb)
        return value, sums

    reset_came, out_came[-1], leave = after((reset_came, out_came[-1], leave), grad_c)
    over = second_start(reset_wg, reset_came)
    send_out(leave[1])
    candidate_wg = weight_part(after(grad_c, over, out_came[0]), "weight_grad_candidate")
    reset_part = after(second_end(reset_wg, reset_came, over), candidate_wg)
    out_came[-1], leave = after((out_came[-1], leave), candidate_wg)
    send_out(leave[2])
    candidate_came = first_sends(after(candidate_wg, reset_part))
    back_far = []
    for dz in range(1, low):
        value, sums = grads_of(low + dz, None, candidate_wg, reset_part, out_came[1])
        back_far.append((value, sums))
    candidate_came, out_came[-1], leave = after((candidate_came, out_came[-1], leave), back_far)
    send_out(leave[3])
    over = second_start(candidate_wg, candidate_came)
    from_core = [(cross_core(value), cross_core(sums)) for value, sums in after(back_far, over)]
    forget_wg = weight_part(after(grad_f, over, back_far, out_came[2]), "weight_grad_forget")
    from_core, out_came[-1] = after((from_core, out_came[-1]), forget_wg)
    candidate_part = after(second_end(candidate_wg, candidate_came, over), forget_wg)
    forget_came = first_sends(after(forget_wg, candidate_part, from_core, out_came))
    if rounds_first := back_routes[0][2]:
        sends = call(
            functools.partial(pick_kernel, "back_stream", info, 2),
            [shape_of((part, channels), BF16)] * rounds_first,
            [full((part, channels))] * 2,
            [full((part, channels))] * rounds_first,
            cost_estimate=cost(0, 3 * part * channels),
            name="pick_parts",
        )(scalars, candidate_part, reset_part)
    first_parts = to_owners(0, sends)
    far_values = []
    for dz in range(1, low):
        value, sums = grads_of(dz, from_core[dz - 1][0], forget_wg, sends)
        far_values.append((value, sums + from_core[dz - 1][1]))
    forget_came = after(forget_came, far_values)
    over = second_start(forget_wg, forget_came)
    value_other, sums_other = grads_of(low, None, over, far_values)
    forget_part = after(second_end(forget_wg, forget_came, over), value_other)
    first_parts = after(first_parts, value_other)
    forget_part = after(forget_part, first_parts)
    last_parts = to_owners(1, [forget_part] * back_routes[1][2])
    value_core, sums_core = cross_core(value_other), cross_core(sums_other)
    value_own, sums_own = grads_of(0, None, forget_part, first_parts)
    last_parts = after(last_parts, value_own)
    far = [
        (cross_low(value, dz + 1), cross_low(sums, dz + 1))
        for dz, (value, sums) in enumerate(after(far_values, last_parts))
    ]
    owned_parts = first_parts + [candidate_part, reset_part] + last_parts + [forget_part]

    block_piece = (3, half, channels)
    own_blocks, give_blocks = call(
        functools.partial(owned_kernel, info, len(owned_parts)),
        [shape_of(block_piece, BF16)] * 2,
        [anywhere] * len(owned_parts),
        [full(block_piece)] * 2,
        scratch=[
            pltpu.VMEM((3, part, channels), F32),
            pltpu.VMEM((len(owned_parts), part, channels), BF16),
            pltpu.SemaphoreType.DMA((len(owned_parts),)),
        ],
        cost_estimate=cost(0, 6 * part * channels),
        name="own_blocks",
    )(scalars, *owned_parts)
    own_sum = add_up([own_blocks, cross_core(give_blocks)])
    whole = [own_sum] + [cross_plane(own_sum, d) for d in (others[:2] if short else others)]
    split = []
    if short:
        split = [cross_plane(whole[1][:, :quarter], 2), cross_plane(whole[2][:, quarter:], 1)]
    whole = whole + [cross_core(value) for value in whole]
    split = split + [cross_core(value) for value in split]

    def spread(name, values, steps, held):
        return call(
            functools.partial(spread_kernel, len(values), steps),
            shape_of((width, 3 * channels), F32),
            [full(value.shape) for value in values] + [anywhere] * len(held),
            pl.BlockSpec((quarter, 3 * channels), lambda t, s: (s[getattr(info, name) + t], 0)),
            grid=(len(steps),),
            aliases={1 + len(values): 0} if held else None,
            cost_estimate=cost(0, 9 * width * channels),
            name="spread_" + name,
        )(scalars, *values, *held)

    weight_grad = spread("whole_rows", whole, [(n, at) for n in range(len(whole)) for at in (0, quarter)], ())
    if short:
        weight_grad = spread("split_rows", split, [(n, 0) for n in range(len(split))], (weight_grad,))
    gate_sums = jnp.sum(jnp.concatenate([forget_sums, reset_sums]), axis=1)
    spread_sums = lax.dynamic_update_slice(
        jnp.zeros((4, width), F32), gate_sums, (0, (z % low + low * k) * channels)
    )
    small = jnp.concatenate([jnp.sum(sum(norm_sums[1:], norm_sums[0]), axis=1), spread_sums], axis=0)
    small = after(small, whole)
    small = small + cross_core(small)
    for bit in bits_of(planes):
        small = small + cross_plane(small, bit)
    for bit in bits_of(groups):
        small = small + cross_low(small, bit)

    came = jnp.stack(out_came).reshape(stay.shape)
    output = jnp.where(zhi == 0, jnp.stack([stay, came]), jnp.stack([came, stay])).reshape(groups * rows, channels)
    far, weight_grad = after((far, weight_grad), weight_grad)
    parts = [value_own, value_core] + [value for value, _ in far]
    sums = sum([sums_core] + [sums for _, sums in far], sums_own)
    input_grad = pl.pallas_call(
        functools.partial(last_kernel, len(parts)),
        grid=(tiles,),
        in_specs=[
            pl.BlockSpec((tile, width), lambda t: (t, 0)),
            pl.BlockSpec((tile, rows), lambda t: (t, 0)),
        ]
        + [full((rows, width))] * len(parts)
        + [full((SUB, rows))],
        out_specs=pl.BlockSpec((tile, width), lambda t: (t, 0)),
        out_shape=shape_of((rows, width), F32),
        compiler_params=params(),
        cost_estimate=cost(4 * rows * rows * width, 10 * rows * width),
        name="input_grad",
    )(inputs, back_order, *parts, sums)
    gate_block = lax.dynamic_slice_in_dim(small[2:], z * channels, channels, 1)
    return (
        output,
        input_grad,
        weight_grad,
        small[0],
        small[1],
        gate_block[1],
        gate_block[3],
        gate_block[0],
        gate_block[2],
    )


def solution(mesh):
    placed = (
        P(("seq", "col"), None),
        P(),
        P(),
        P(None, "col"),
        P("col"),
        P("col"),
        P("col"),
        P("col"),
        P(),
        P("seq", "col"),
    )
    return jax.shard_map(
        per_device,
        mesh=mesh,
        in_specs=placed,
        out_specs=(
            P("seq", "col"),
            P(("seq", "col"), None),
            P(None, "col"),
            P(),
            P(),
            P("col"),
            P("col"),
            P("col"),
            P("col"),
        ),
        check_vma=False,
    )
```

time: 2020 us -> 433 us (0.21)
  waiting for transfers between devices: 853 us -> 118 us
  local copies, waits for them, and re-layouts: 633 us -> 19.3 us
  blocking collectives: 227 us -> 0 us
  Pallas kernels: 0 us -> 186 us
  other arithmetic: 147 us -> 12.6 us
  matrix products: 57 us -> 1.26 us
    all_gather x2 -> x1, waiting for transfers between devices: 423 us -> 0.02 us  [per_device(): lax.all_gather(value, 'seq', axis_index_groups=plane_groups, tiled=True)]
    slice x156 -> x10, local copies, waits for them, and re-layouts: 276 us -> 4.05 us  [the longest x1 1.24 us: per_device(): permuted[tile:]]
    reduce_scatter x2 -> x0, waiting for transfers between devices: 220 us -> none  [the longest x1 158 us: per_device(): lax.psum_scatter(lax.dot_general(ordered, normed_low, (((0,), (0,)), ((),...]
    pallas_call x0 -> x21, Pallas kernels: none -> 186 us  [the longest x4 41.8 us: chunk_grad(): call(functools.partial(input_kernel, info, joined is not None), (shape_of...]
    all_to_all x1 -> x0, blocking collectives: 184 us -> none  [per_device(): lax.all_to_all(stream_grads[:, :, None, :], 'col', split_axis=0, concat_a...]
    all_to_all x3 -> x0, waiting for transfers between devices: 173 us -> none  [the longest x1 128 us: per_device(): lax.all_to_all(mixed_low, 'col', split_axis=2, concat_axis=0, tiled=True)]
    pad x80 -> x0, local copies, waits for them, and re-layouts: 170 us -> none  [the longest x40 85.3 us: per_device(): lax.associative_scan(compose, (back_decay[::-1], back_inject[::-1]), axis=0)]
    ppermute x14 -> x69, waiting for transfers between devices: 36.1 us -> 118 us  [move(): return lax.ppermute(value, ('seq', 'col'), pairs)]
  transfers between devices with their start and end apart: 21 -> 70, of which waited for: 19 -> 23; matrix products, arithmetic and copies ran while one was open for 17% -> 4% of each run, Pallas kernels for 0% -> 37%
where the time goes in v1:
time: 433 us; the launch traced here: 428 us
  Pallas kernels  186 us (43%)
  waiting for transfers between devices  118 us (27%)
  starting transfers between devices  75.5 us (17%)
  local copies, waits for them, and re-layouts  19.3 us (4%)
  between operations  15.1 us (3%)
  other arithmetic  12.6 us (3%)
    ppermute x69, waiting for transfers between devices, move(): return lax.ppermute(value, ('seq', 'col'), pairs)  118 us
    ppermute x69, starting transfers between devices, move(): return lax.ppermute(value, ('seq', 'col'), pairs)  75.5 us
    pallas_call x4, Pallas kernels, chunk_grad(): call(functools.partial(input_kernel, info, joined is not None), (shape_of...  41.8 us
    pallas_call x3, Pallas kernels, weight_part(): call(functools.partial(weight_grad_kernel, places), [shape_of(shape, BF16...  29.9 us
    pallas_call x1, Pallas kernels, per_device(): call(functools.partial(state_kernel, info, low, planes, seg), (shape_of(r...  18.9 us
    pallas_call x1, Pallas kernels, per_device(): call(functools.partial(mix_far_kernel, info, low, seg, far_order, tile),...  18.3 us
    pallas_call x1, Pallas kernels, per_device(): call(functools.partial(mix_kernel, info, low, planes, seg, here, away, sh...  14.8 us
    pallas_call x2, Pallas kernels, spread(): call(functools.partial(spread_kernel, len(values), steps), shape_of((widt...  13.3 us
  transfers between devices with their start and end apart: 70, of which 23 were waited for; matrix products, arithmetic and copies ran while one was open for 4% of the time, Pallas kernels for 37%

profile of v1, /device:TPU:12, one launch (start us, length us, event | category | flops | bytes accessed | tf_op | source)
XLA Modules:
  0.0 428.3 jit_solution(17562285732391590093)
XLA Ops:
  8.4 4.1 cut_weight.2
  19.9 4.4 %collective-permute-start.3 = (bf16[512,512]{1,0:T(8,128)(2,1)}, bf16[512,512]{1,0:T(8,128)(2,1)}, u32[]{:S(2)}, u32[]{:S(2)}) collective-permute-start(bf16[512,512]{1,0:T(8,128)(2,1)} %get-tuple-element.141), channel_id=1, source_target_pairs={{0,2},{1,0},{3,1},{6,4},{7,5},{8,10},{9,8},{11,9},{14,12},{15,13},... | collective-permute-start | bytes 1572872 | tf_op jit(solution)/shard_map/ppermute | solution.py:609
  34.9 14.5 %collective-permute-done.2.refs_0_ = bf16[512,512]{1,0:T(8,128)(2,1)S(1)} collective-permute-done((bf16[512,512]{1,0:T(8,128)(2,1)}, bf16[512,512]{1,0:T(8,128)(2,1)S(1)}, u32[]{:S(2)}, u32[]{:S(2)}) %collective-permute-start.2) | collective-permute-done | bytes 524320 | tf_op jit(solution)/shard_map/ppermute | solution.py:609
  49.4 5.9 %collective-permute-done.4.refs_2_ = bf16[512,512]{1,0:T(8,128)(2,1)} collective-permute-done((bf16[512,512]{1,0:T(8,128)(2,1)}, bf16[512,512]{1,0:T(8,128)(2,1)}, u32[]{:S(2)}, u32[]{:S(2)}) %collective-permute-start.4) | collective-permute-done | bytes 524320 | tf_op jit(solution)/shard_map/ppermute | solution.py:609
  60.7 20.9 %collective-permute-done.6.refs_2_ = bf16[2,512,512]{2,1,0:T(8,128)(2,1)S(1)} collective-permute-done((bf16[2,512,512]{2,1,0:T(8,128)(2,1)}, bf16[2,512,512]{2,1,0:T(8,128)(2,1)S(1)}, u32[]{:S(2)}, u32[]{:S(2)}) %collective-permute-start.6) | collective-permute-done | bytes 1048608 | tf_op jit(solution)/shard_map/ppermute | solution.py:609
  84.7 5.4 %collective-permute-start.11 = (bf16[256,512]{1,0:T(8,128)(2,1)}, bf16[256,512]{1,0:T(8,128)(2,1)S(1)}, u32[]{:S(2)}, u32[]{:S(2)}) collective-permute-start(bf16[256,512]{1,0:T(8,128)(2,1)} %constant_dynamic-slice_fusion.3), channel_id=1, source_target_pairs={{0,2},{1,3},{2,0},{3,1},{4,6},{5,7},{6,4},{7,5},{8,10},{9,11},{10,... | collective-permute-start | bytes 786440 | tf_op jit(solution)/shard_map/ppermute | solution.py:609
  90.1 5.0 %norm_chunk.2 = (bf16[4,512,2048]{2,1,0:T(8,128)(2,1)}, bf16[4,512,512]{2,1,0:T(8,128)(2,1)}, bf16[4,512,2048]{2,1,0:T(8,128)(2,1)}, f32[4,512,128]{2,1,0:T(8,128)}) custom-call(s32[52]{0:T(128)} %fusion.13.s, bf16[512,2048]{1,0:T(8,128)(2,1)} %copy-done, f32[1,2048]{1,0:T(1,128)} %bitcast.89, f32[1,2048]{1,0:T(1,128)} %bitcast.104), custom_call_target="tpu_custom_call" | custom-call | flops 12582912 | bytes 7340032 | tf_op jit(solution)/shard_map/norm_chunk/pallas_call | solution.py:793
  95.2 5.1 %norm_chunk.3 = (bf16[4,512,2048]{2,1,0:T(8,128)(2,1)}, bf16[4,512,512]{2,1,0:T(8,128)(2,1)}, bf16[4,512,2048]{2,1,0:T(8,128)(2,1)}, f32[4,512,128]{2,1,0:T(8,128)}) custom-call(s32[52]{0:T(128)} %fusion.13.s, bf16[512,2048]{1,0:T(8,128)(2,1)} %collective-permute-done.x_ref, ...), custom_call_target="tpu_custom_call", output_to_operand_aliasing={{0}: (4, {}), {1}: (5, {}), {2}: (6, {}), {3}: (7, {})} | custom-call | flops 12582912 | bytes 7340032 | tf_op jit(solution)/shard_map/norm_chunk/pallas_call | solution.py:793
  100.2 3.7 collective-permute-done.11
  106.6 14.8 %mix_near.1 = (bf16[4,3,512,512]{3,2,1,0:T(8,128)(2,1)}, f32[4,2,8,512]{3,2,1,0:T(8,128)}, bf16[3,2048,512]{2,1,0:T(8,128)(2,1)}) custom-call(s32[52]{0:T(128)} %fusion.13.s, s32[4]{0:T(128)} %lengths.7, bf16[4,512,2048]{2,1,0:T(8,128)(2,1)} %get-tuple-element.148.normed_ref.refs_4_, f32[1,512]{1,0:T(1,128)} %get-tuple-element.284.fp_ref.refs_12_.refs_16_, ...), custom_call_target="tpu_custom_call" | custom-call | flops 6442450944 | bytes 29360128 | tf_op jit(solution)/shard_map/mix_near/pallas_call | solution.py:817
  127.0 18.3 %mix_far.1 = (bf16[4,512,2048]{2,1,0:T(8,128)(2,1)}, bf16[4,512,512]{2,1,0:T(8,128)(2,1)}, bf16[4,512,2048]{2,1,0:T(8,128)(2,1)}, f32[4,512,128]{2,1,0:T(8,128)}...) custom-call(s32[52]{0:T(128)} %fusion.13.s, ...), custom_call_target="tpu_custom_call", output_to_operand_aliasing={{0}: (12, {}), {1}: (13, {}), {2}: (14, {}), {3}: (15, {}),... | custom-call | flops 6442450944 | bytes 29360128 | tf_op jit(solution)/shard_map/mix_far/pallas_call | solution.py:843
  154.6 5.1 %collective-permute-done.18.refs_4_ = f32[4,8,512]{2,1,0:T(8,128)S(1)} collective-permute-done((f32[4,8,512]{2,1,0:T(8,128)S(1)}, f32[4,8,512]{2,1,0:T(8,128)S(1)}, u32[]{:S(2)}, u32[]{:S(2)}) %collective-permute-start.18) | collective-permute-done | bytes 65568 | tf_op jit(solution)/shard_map/ppermute | solution.py:609
  160.7 18.9 %states.1 = (bf16[2,512,512]{2,1,0:T(8,128)(2,1)}, bf16[2,512,512]{2,1,0:T(8,128)(2,1)}, f32[4,512,512]{2,1,0:T(8,128)}, f32[4,512,512]{2,1,0:T(8,128)}, f32[4,5...) custom-call(s32[52]{0:T(128)} %fusion.13.s, ...), custom_call_target="tpu_custom_call" | custom-call | flops 62914560 | bytes 31457280 | tf_op jit(solution)/shard_map/states/pallas_call | solution.py:886
  188.6 10.1 %weight_grad_reset.1 = (bf16[2,256,512]{2,1,0:T(8,128)(2,1)}, bf16[2,256,512]{2,1,0:T(8,128)(2,1)}, bf16[2,256,512]{2,1,0:T(8,128)(2,1)}, bf16[2,256,512]{2,1,0:T(8,128)(2,1)}) custom-call(s32[52]{0:T(128)} %fusion.13.s, bf16[4,512,2048]{2,1,0:T(8,128)(2,1)} %get-tuple-element.178.normed_ref, bf16[4,512,512]{2,1,0:T(8,128)(2,1)} %get-tuple-element.181.grads_ref.rzb_ref), custom_call_target="tpu_custom_call" | custom-call | flops 4294967296 | bytes 16777216 | tf_op jit(solution)/shard_map/weight_grad_reset/pallas_call | solution.py:938
  202.7 12.3 %state_grads.1 = (bf16[4,512,512]{2,1,0:T(8,128)(2,1)}, bf16[4,512,512]{2,1,0:T(8,128)(2,1)}, f32[2,8,512]{2,1,0:T(8,128)}) custom-call(s32[52]{0:T(128)} %fusion.13.s, s32[4]{0:T(128)} %lengths.7, f32[8,512]{1,0:T(8,128)} %get-tuple-element.168.refs_0_, f32[8,512]{1,0:T(8,128)} %copy-done.42, f32[8,512]{1,0:T(8,128)} %copy-done.40, f32[8,512]{1,0:T(8,128)} %copy-done.41, ...), custom_call_target="tpu_custom_call" | custom-call | flops 31457280 | bytes 20971520 | tf_op jit(solution)/shard_map/state_grads/pallas_call | solution.py:991
  218.4 9.9 %weight_grad_candidate.1 = (bf16[2,256,512]{2,1,0:T(8,128)(2,1)}, bf16[2,256,512]{2,1,0:T(8,128)(2,1)}, bf16[2,256,512]{2,1,0:T(8,128)(2,1)}, bf16[2,256,512]{2,1,0:T(8,128)(2,1)}) custom-call(s32[52]{0:T(128)} %fusion.13.s, bf16[4,512,2048]{2,1,0:T(8,128)(2,1)} %get-tuple-element.178.normed_ref, bf16[4,512,512]{2,1,0:T(8,128)(2,1)} %get-tuple-element.250.grads_ref.grad_c_ref), custom_call_target="tpu_custom_call" | custom-call | flops 4294967296 | bytes 16777216 | tf_op jit(solution)/shard_map/weight_grad_candidate/pallas_call | solution.py:938
  231.7 5.5 %collective-permute-done.29 = bf16[256,512]{1,0:T(8,128)(2,1)S(1)} collective-permute-done((bf16[256,512]{1,0:T(8,128)(2,1)S(1)}, bf16[256,512]{1,0:T(8,128)(2,1)S(1)}, u32[]{:S(2)}, u32[]{:S(2)}) %collective-permute-start.29) | collective-permute-done | bytes 262176 | tf_op jit(solution)/shard_map/ppermute | solution.py:609
  240.7 10.3 %chunk_grad.4 = (bf16[512,2048]{1,0:T(8,128)(2,1)}, f32[8,512]{1,0:T(8,128)}, f32[2,8,2048]{2,1,0:T(8,128)}) custom-call(s32[52]{0:T(128)} %fusion.13.s, bf16[4,512,512]{2,1,0:T(8,128)(2,1)} %get-tuple-element.250.grads_ref.grad_c_ref, bf16[4,512,512]{2,1,0:T(8,128)(2,1)} %get-tuple-element.224.grad_f_ref.grads_ref, ...), custom_call_target="tpu_custom_call" | custom-call | flops 3221225472 | bytes 14680064 | tf_op jit(solution)/shard_map/chunk_grad/pallas_call | solution.py:1021
  253.4 9.9 %weight_grad_forget.1 = (bf16[2,256,512]{2,1,0:T(8,128)(2,1)}, bf16[2,256,512]{2,1,0:T(8,128)(2,1)}, bf16[2,256,512]{2,1,0:T(8,128)(2,1)}, bf16[2,256,512]{2,1,0:T(8,128)(2,1)}) custom-call(s32[52]{0:T(128)} %fusion.13.s, bf16[4,512,2048]{2,1,0:T(8,128)(2,1)} %get-tuple-element.178.normed_ref, bf16[4,512,512]{2,1,0:T(8,128)(2,1)} %get-tuple-element.224.grad_f_ref.grads_ref), custom_call_target="tpu_custom_call" | custom-call | flops 4294967296 | bytes 16777216 | tf_op jit(solution)/shard_map/weight_grad_forget/pallas_call | solution.py:938
  265.6 10.7 %collective-permute-done.37 = bf16[256,512]{1,0:T(8,128)(2,1)S(1)} collective-permute-done((bf16[256,512]{1,0:T(8,128)(2,1)S(1)}, bf16[256,512]{1,0:T(8,128)(2,1)S(1)}, u32[]{:S(2)}, u32[]{:S(2)}) %collective-permute-start.37) | collective-permute-done | bytes 262176 | tf_op jit(solution)/shard_map/ppermute | solution.py:609
  282.7 5.3 %collective-permute-start.44 = (bf16[512,512]{1,0:T(8,128)(2,1)}, bf16[512,512]{1,0:T(8,128)(2,1)S(1)}, u32[]{:S(2)}, u32[]{:S(2)}) collective-permute-start(bf16[512,512]{1,0:T(8,128)(2,1)} %get-tuple-element.231), channel_id=1, source_target_pairs={{0,2},{1,3},{2,0},{4,7},{6,4},{7,5},{8,10},{9,11},{10,8},{12,15},{... | collective-permute-start | bytes 1572872 | tf_op jit(solution)/shard_map/ppermute | solution.py:609
  291.1 11.1 %chunk_grad.5 = (bf16[512,2048]{1,0:T(8,128)(2,1)}, f32[8,512]{1,0:T(8,128)}, f32[2,8,2048]{2,1,0:T(8,128)}) custom-call(s32[52]{0:T(128)} %fusion.13.s, bf16[4,512,512]{2,1,0:T(8,128)(2,1)} %get-tuple-element.250.grads_ref.grad_c_ref, bf16[4,512,512]{2,1,0:T(8,128)(2,1)} %get-tuple-element.224.grad_f_ref.grads_ref, ...), custom_call_target="tpu_custom_call" | custom-call | flops 3221225472 | bytes 14680064 | tf_op jit(solution)/shard_map/chunk_grad/pallas_call | solution.py:1021
  304.7 10.2 %chunk_grad.6 = (bf16[512,2048]{1,0:T(8,128)(2,1)}, f32[8,512]{1,0:T(8,128)}, f32[2,8,2048]{2,1,0:T(8,128)}) custom-call(s32[52]{0:T(128)} %fusion.13.s, bf16[4,512,512]{2,1,0:T(8,128)(2,1)} %get-tuple-element.250.grads_ref.grad_c_ref, bf16[4,512,512]{2,1,0:T(8,128)(2,1)} %get-tuple-element.224.grad_f_ref.grads_ref, ...), custom_call_target="tpu_custom_call" | custom-call | flops 3221225472 | bytes 14680064 | tf_op jit(solution)/shard_map/chunk_grad/pallas_call | solution.py:1021
  319.1 10.2 %chunk_grad.7 = (bf16[512,2048]{1,0:T(8,128)(2,1)}, f32[8,512]{1,0:T(8,128)}, f32[2,8,2048]{2,1,0:T(8,128)}) custom-call(s32[52]{0:T(128)} %fusion.13.s, bf16[4,512,512]{2,1,0:T(8,128)(2,1)} %get-tuple-element.250.grads_ref.grad_c_ref, bf16[4,512,512]{2,1,0:T(8,128)(2,1)} %get-tuple-element.224.grad_f_ref.grads_ref, ...), custom_call_target="tpu_custom_call" | custom-call | flops 3221225472 | bytes 14680064 | tf_op jit(solution)/shard_map/chunk_grad/pallas_call | solution.py:1021
  329.7 3.5 collective-permute-done.49.refs_6_
  334.2 3.6 own_blocks.1
  344.9 16.5 %collective-permute-done.54.refs_1_ = bf16[3,256,512]{2,1,0:T(8,128)(2,1)S(1)} collective-permute-done((bf16[3,256,512]{2,1,0:T(8,128)(2,1)S(1)}, bf16[3,256,512]{2,1,0:T(8,128)(2,1)S(1)}, u32[]{:S(2)}, u32[]{:S(2)}) %collective-permute-start.54) | collective-permute-done | bytes 786464 | tf_op jit(solution)/shard_map/ppermute | solution.py:609
  364.8 7.2 %collective-permute-done.55.refs_0_ = bf16[3,128,512]{2,1,0:T(8,128)(2,1)} collective-permute-done((bf16[3,128,512]{2,1,0:T(8,128)(2,1)S(1)}, bf16[3,128,512]{2,1,0:T(8,128)(2,1)}, u32[]{:S(2)}, u32[]{:S(2)}) %collective-permute-start.55) | collective-permute-done | bytes 393248 | tf_op jit(solution)/shard_map/ppermute | solution.py:609
  375.0 6.9 %collective-permute-done.57.refs_1_ = bf16[3,128,512]{2,1,0:T(8,128)(2,1)} collective-permute-done((bf16[3,128,512]{2,1,0:T(8,128)(2,1)}, bf16[3,128,512]{2,1,0:T(8,128)(2,1)}, u32[]{:S(2)}, u32[]{:S(2)}) %collective-permute-start.57) | collective-permute-done | bytes 393248 | tf_op jit(solution)/shard_map/ppermute | solution.py:609
  391.5 9.0 %spread_whole_rows.1.refs_4_ = f32[2048,1536]{1,0:T(8,128)} custom-call(s32[52]{0:T(128)} %fusion.13.s, bf16[3,256,512]{2,1,0:T(8,128)(2,1)} %copy-done.1, bf16[3,256,512]{2,1,0:T(8,128)(2,1)} %copy-done.6, bf16[3,256,512]{2,1,0:T(8,128)(2,1)} %copy-done.7, bf16[3,256,512]{2,1,0:T(8,128)(2,1)} %copy-done.13, ...), custom_call_target="tpu_custom_call" | custom-call | bytes 9437184 | tf_op jit(solution)/shard_map/spread_whole_rows/pallas_call | solution.py:1135
  400.5 4.3 %spread_split_rows.1 = f32[2048,1536]{1,0:T(8,128)} custom-call(s32[52]{0:T(128)} %fusion.13.s, bf16[3,128,512]{2,1,0:T(8,128)(2,1)} %collective-permute-done.55.refs_0_, bf16[3,128,512]{2,1,0:T(8,128)(2,1)} %collective-permute-done.57.refs_1_, bf16[3,128,512]{2,1,0:T(8,128)(2,1)} %collective-permute-done.58.refs_2_, ...), custom_call_target="tpu_custom_call", output_to_operand_aliasing={{}: (5, {})} | custom-call | bytes 9437184 | tf_op jit(solution)/shard_map/spread_split_rows/pallas_call | solution.py:1135
  409.9 10.2 %input_grad.1 = f32[512,2048]{1,0:T(8,128)} custom-call(bf16[512,2048]{1,0:T(8,128)(2,1)} %x_ref.1, bf16[512,512]{1,0:T(8,128)(2,1)} %constant.71.clone.refs_11_.order_ref, bf16[512,2048]{1,0:T(8,128)(2,1)} %get-tuple-element.251.refs_0_, bf16[512,2048]{1,0:T(8,128)(2,1)} %collective-permute-done.47.refs_1_, ...), custom_call_target="tpu_custom_call" | custom-call | flops 2147483648 | bytes 10485760 | tf_op jit(solution)/shard_map/input_grad/pallas_call | solution.py:1166
  (308 shorter events, 120.4 us)
Async XLA Ops:
  7.2 51.5 %all-gather.2.cloned.1.call-start = ((), (), s32[]{:S(2)}) async-start(), calls=%async_computation | async-start | bytes 2621440 | tf_op jit(solution)/shard_map/all_gather | solution.py:745
  16.5 32.8 %collective-permute-start.2 = (bf16[512,512]{1,0:T(8,128)(2,1)}, bf16[512,512]{1,0:T(8,128)(2,1)S(1)}, u32[]{:S(2)}, u32[]{:S(2)}) collective-permute-start(bf16[512,512]{1,0:T(8,128)(2,1)} %get-tuple-element.140), channel_id=1, source_target_pairs={{0,3},{1,2},{2,0},{4,6},{5,7},{6,5},{7,4},{8,11},{9,10},{10,8},{12... | collective-permute-start | bytes 1572872 | tf_op jit(solution)/shard_map/ppermute | solution.py:609
  19.9 29.5 %collective-permute-start.3 = (bf16[512,512]{1,0:T(8,128)(2,1)}, bf16[512,512]{1,0:T(8,128)(2,1)}, u32[]{:S(2)}, u32[]{:S(2)}) collective-permute-start(bf16[512,512]{1,0:T(8,128)(2,1)} %get-tuple-element.141), channel_id=1, source_target_pairs={{0,2},{1,0},{3,1},{6,4},{7,5},{8,10},{9,8},{11,9},{14,12},{15,13},... | collective-permute-start | bytes 1572872 | tf_op jit(solution)/shard_map/ppermute | solution.py:609
  24.3 31.0 %collective-permute-start.4 = (bf16[512,512]{1,0:T(8,128)(2,1)}, bf16[512,512]{1,0:T(8,128)(2,1)}, u32[]{:S(2)}, u32[]{:S(2)}) collective-permute-start(bf16[512,512]{1,0:T(8,128)(2,1)} %get-tuple-element.142), channel_id=1, source_target_pairs={{0,1},{1,3},{6,7},{7,6},{8,9},{9,11},{14,15},{15,14},{16,17},{17,1... | collective-permute-start | bytes 1572872 | tf_op jit(solution)/shard_map/ppermute | solution.py:609
  27.5 31.1 %collective-permute-start.5 = (bf16[128,2048]{1,0:T(8,128)(2,1)S(1)}, bf16[128,2048]{1,0:T(8,128)(2,1)}, u32[]{:S(2)}, u32[]{:S(2)}) collective-permute-start(bf16[128,2048]{1,0:T(8,128)(2,1)S(1)} %slice.183), channel_id=1, source_target_pairs={{0,1},{1,0},{2,3},{3,2},{4,5},{5,4},{6,7},{7,6},{8,9},{9,8},{10,11... | collective-permute-start | bytes 1572872 | tf_op jit(solution)/shard_map/ppermute | solution.py:609
  32.0 26.6 %collective-permute-start.1 = (f32[4,512]{1,0:T(4,128)S(1)}, f32[4,512]{1,0:T(4,128)S(1)}, u32[]{:S(2)}, u32[]{:S(2)}) collective-permute-start(f32[4,512]{1,0:T(4,128)S(1)} %pad_maximum_fusion.7), channel_id=1, source_target_pairs={{0,2},{1,3},{2,0},{3,1},{4,6},{5,7},{6,4},{7,5},{8,10},{9,11},{10,... | collective-permute-start | bytes 24584 | tf_op jit(solution)/shard_map/ppermute | solution.py:609
  58.7 23.0 %collective-permute-start.6 = (bf16[2,512,512]{2,1,0:T(8,128)(2,1)}, bf16[2,512,512]{2,1,0:T(8,128)(2,1)S(1)}, u32[]{:S(2)}, u32[]{:S(2)}) collective-permute-start(bf16[2,512,512]{2,1,0:T(8,128)(2,1)} %pick_blocks.1.refs_1_), channel_id=1, source_target_pairs={{0,8},{1,9},{2,10},{3,11},{4,12},{5,13},{6,14},{7,15},{8,0},{9,1},... | collective-permute-start | bytes 3145736 | tf_op jit(solution)/shard_map/ppermute | solution.py:609
  60.2 24.4 %collective-permute-start.7 = (bf16[2,512,512]{2,1,0:T(8,128)(2,1)}, bf16[2,512,512]{2,1,0:T(8,128)(2,1)S(1)}, u32[]{:S(2)}, u32[]{:S(2)}) collective-permute-start(bf16[2,512,512]{2,1,0:T(8,128)(2,1)} %pick_blocks.1.refs_1_), channel_id=1, source_target_pairs={{0,16},{1,17},{2,18},{3,19},{4,20},{5,21},{6,22},{7,23},{8,24},{9,... | collective-permute-start | bytes 3145736 | tf_op jit(solution)/shard_map/ppermute | solution.py:609
  60.7 43.2 %collective-permute-start.10 = (bf16[384,2048]{1,0:T(8,128)(2,1)S(1)}, bf16[384,2048]{1,0:T(8,128)(2,1)S(1)}, u32[]{:S(2)}, u32[]{:S(2)}) collective-permute-start(bf16[384,2048]{1,0:T(8,128)(2,1)S(1)} %copy-done.8), channel_id=1, source_target_pairs={{0,1},{1,0},{2,3},{3,2},{4,5},{5,4},{6,7},{7,6},{8,9},{9,8},{10,11... | collective-permute-start | bytes 4718600 | tf_op jit(solution)/shard_map/ppermute | solution.py:609
  81.7 22.2 %collective-permute-start.8 = (bf16[2,256,512]{2,1,0:T(8,128)(2,1)S(1)}, bf16[2,256,512]{2,1,0:T(8,128)(2,1)S(1)}, u32[]{:S(2)}, u32[]{:S(2)}) collective-permute-start(bf16[2,256,512]{2,1,0:T(8,128)(2,1)S(1)} %slice.184), channel_id=1, source_target_pairs={{0,16},{1,17},{2,18},{3,19},{4,20},{5,21},{6,22},{7,23},{8,24},{9,... | collective-permute-start | bytes 1572872 | tf_op jit(solution)/shard_map/ppermute | solution.py:609
  84.6 19.3 %collective-permute-start.9 = (bf16[2,256,512]{2,1,0:T(8,128)(2,1)S(1)}, bf16[2,256,512]{2,1,0:T(8,128)(2,1)S(1)}, u32[]{:S(2)}, u32[]{:S(2)}) collective-permute-start(bf16[2,256,512]{2,1,0:T(8,128)(2,1)S(1)} %slice.185), channel_id=1, source_target_pairs={{0,8},{1,9},{2,10},{3,11},{4,12},{5,13},{6,14},{7,15},{8,0},{9,1},... | collective-permute-start | bytes 1572872 | tf_op jit(solution)/shard_map/ppermute | solution.py:609
  84.7 19.2 %collective-permute-start.11 = (bf16[256,512]{1,0:T(8,128)(2,1)}, bf16[256,512]{1,0:T(8,128)(2,1)S(1)}, u32[]{:S(2)}, u32[]{:S(2)}) collective-permute-start(bf16[256,512]{1,0:T(8,128)(2,1)} %constant_dynamic-slice_fusion.3), channel_id=1, source_target_pairs={{0,2},{1,3},{2,0},{3,1},{4,6},{5,7},{6,4},{7,5},{8,10},{9,11},{10,... | collective-permute-start | bytes 786440 | tf_op jit(solution)/shard_map/ppermute | solution.py:609
  105.0 20.7 %collective-permute-start.13 = (bf16[384,2048]{1,0:T(8,128)(2,1)S(1)}, bf16[384,2048]{1,0:T(8,128)(2,1)S(1)}, u32[]{:S(2)}, u32[]{:S(2)}) collective-permute-start(bf16[384,2048]{1,0:T(8,128)(2,1)S(1)} %collective-permute-done.10.refs_1_), channel_id=1, source_target_pairs={{0,4},{1,5},{2,6},{3,7},{4,0},{5,1},{6,2},{7,3},{8,12},{9,13},{10,... | collective-permute-start | bytes 4718600 | tf_op jit(solution)/shard_map/ppermute | solution.py:609
  106.5 19.2 %collective-permute-start.12 = (bf16[128,2048]{1,0:T(8,128)(2,1)}, bf16[128,2048]{1,0:T(8,128)(2,1)S(1)}, u32[]{:S(2)}, u32[]{:S(2)}) collective-permute-start(bf16[128,2048]{1,0:T(8,128)(2,1)} %collective-permute-done.5.refs_0_), channel_id=1, source_target_pairs={{0,4},{1,5},{2,6},{3,7},{4,0},{5,1},{6,2},{7,3},{8,12},{9,13},{10,... | collective-permute-start | bytes 1572872 | tf_op jit(solution)/shard_map/ppermute | solution.py:609
  122.3 23.0 %collective-permute-start.19 = (bf16[416,512]{1,0:T(8,128)(2,1)S(1)}, bf16[416,512]{1,0:T(8,128)(2,1)S(1)}, u32[]{:S(2)}, u32[]{:S(2)}) collective-permute-start(bf16[416,512]{1,0:T(8,128)(2,1)S(1)} %copy-done.29), channel_id=1, source_target_pairs={{0,2},{1,3},{2,0},{3,1},{4,6},{5,7},{6,4},{7,5},{8,10},{9,11},{10,... | collective-permute-start | bytes 1277960 | tf_op jit(solution)/shard_map/ppermute | solution.py:609
  179.6 20.7 %collective-permute-start.21 = (bf16[2,512,512]{2,1,0:T(8,128)(2,1)}, bf16[2,512,512]{2,1,0:T(8,128)(2,1)S(1)}, u32[]{:S(2)}, u32[]{:S(2)}) collective-permute-start(bf16[2,512,512]{2,1,0:T(8,128)(2,1)} %get-tuple-element.177), channel_id=1, source_target_pairs={{0,4},{1,5},{2,6},{3,7},{4,0},{5,1},{6,2},{7,3},{8,12},{9,13},{10,... | collective-permute-start | bytes 3145736 | tf_op jit(solution)/shard_map/ppermute | solution.py:609
  230.3 20.8 %collective-permute-start.32 = (bf16[2,256,512]{2,1,0:T(8,128)(2,1)S(1)}, bf16[2,256,512]{2,1,0:T(8,128)(2,1)S(1)}, u32[]{:S(2)}, u32[]{:S(2)}) collective-permute-start(bf16[2,256,512]{2,1,0:T(8,128)(2,1)S(1)} %copy-done.57), channel_id=1, source_target_pairs={{0,8},{1,9},{2,10},{3,11},{4,12},{5,13},{6,14},{7,15},{8,0},{9,1},... | collective-permute-start | bytes 1572872 | tf_op jit(solution)/shard_map/ppermute | solution.py:609
  230.8 20.3 %collective-permute-start.33 = (bf16[2,256,512]{2,1,0:T(8,128)(2,1)S(1)}, bf16[2,256,512]{2,1,0:T(8,128)(2,1)S(1)}, u32[]{:S(2)}, u32[]{:S(2)}) collective-permute-start(bf16[2,256,512]{2,1,0:T(8,128)(2,1)S(1)} %copy-done.56), channel_id=1, source_target_pairs={{0,16},{1,17},{2,18},{3,19},{4,20},{5,21},{6,22},{7,23},{8,24},{9,... | collective-permute-start | bytes 1572872 | tf_op jit(solution)/shard_map/ppermute | solution.py:609
  251.8 24.5 %collective-permute-start.35 = (bf16[512,2048]{1,0:T(8,128)(2,1)}, bf16[512,2048]{1,0:T(8,128)(2,1)S(1)}, u32[]{:S(2)}, u32[]{:S(2)}) collective-permute-start(bf16[512,2048]{1,0:T(8,128)(2,1)} %get-tuple-element.221), channel_id=1, source_target_pairs={{0,4},{1,5},{2,6},{3,7},{4,0},{5,1},{6,2},{7,3},{8,12},{9,13},{10,... | collective-permute-start | bytes 6291464 | tf_op jit(solution)/shard_map/ppermute | solution.py:609
  277.0 25.9 %collective-permute-start.40 = (bf16[2,256,512]{2,1,0:T(8,128)(2,1)}, bf16[2,256,512]{2,1,0:T(8,128)(2,1)S(1)}, u32[]{:S(2)}, u32[]{:S(2)}) collective-permute-start(bf16[2,256,512]{2,1,0:T(8,128)(2,1)} %get-tuple-element.237), channel_id=1, source_target_pairs={{0,8},{1,9},{2,10},{3,11},{4,12},{5,13},{6,14},{7,15},{8,0},{9,1},... | collective-permute-start | bytes 1572872 | tf_op jit(solution)/shard_map/ppermute | solution.py:609
  278.0 24.9 %collective-permute-start.41 = (bf16[2,256,512]{2,1,0:T(8,128)(2,1)S(1)}, bf16[2,256,512]{2,1,0:T(8,128)(2,1)S(1)}, u32[]{:S(2)}, u32[]{:S(2)}) collective-permute-start(bf16[2,256,512]{2,1,0:T(8,128)(2,1)S(1)} %copy-done.53), channel_id=1, source_target_pairs={{0,16},{1,17},{2,18},{3,19},{4,20},{5,21},{6,22},{7,23},{8,24},{9,... | collective-permute-start | bytes 1572872 | tf_op jit(solution)/shard_map/ppermute | solution.py:609
  282.7 32.1 %collective-permute-start.44 = (bf16[512,512]{1,0:T(8,128)(2,1)}, bf16[512,512]{1,0:T(8,128)(2,1)S(1)}, u32[]{:S(2)}, u32[]{:S(2)}) collective-permute-start(bf16[512,512]{1,0:T(8,128)(2,1)} %get-tuple-element.231), channel_id=1, source_target_pairs={{0,2},{1,3},{2,0},{4,7},{6,4},{7,5},{8,10},{9,11},{10,8},{12,15},{... | collective-permute-start | bytes 1572872 | tf_op jit(solution)/shard_map/ppermute | solution.py:609
  288.1 26.8 %collective-permute-start.45 = (bf16[512,512]{1,0:T(8,128)(2,1)}, bf16[512,512]{1,0:T(8,128)(2,1)S(1)}, u32[]{:S(2)}, u32[]{:S(2)}) collective-permute-start(bf16[512,512]{1,0:T(8,128)(2,1)} %get-tuple-element.232), channel_id=1, source_target_pairs={{1,0},{5,7},{9,8},{13,15},{17,16},{21,23},{25,24},{29,31}} | collective-permute-start | bytes 1572872 | tf_op jit(solution)/shard_map/ppermute | solution.py:609
  290.3 24.6 %collective-permute-start.46 = (bf16[512,512]{1,0:T(8,128)(2,1)}, bf16[512,512]{1,0:T(8,128)(2,1)S(1)}, u32[]{:S(2)}, u32[]{:S(2)}) collective-permute-start(bf16[512,512]{1,0:T(8,128)(2,1)} %get-tuple-element.233), channel_id=1, source_target_pairs={{3,0},{6,7},{11,8},{14,15},{19,16},{22,23},{27,24},{30,31}} | collective-permute-start | bytes 1572872 | tf_op jit(solution)/shard_map/ppermute | solution.py:609
  341.8 19.6 %collective-permute-start.54 = (bf16[3,256,512]{2,1,0:T(8,128)(2,1)S(1)}, bf16[3,256,512]{2,1,0:T(8,128)(2,1)S(1)}, u32[]{:S(2)}, u32[]{:S(2)}) collective-permute-start(bf16[3,256,512]{2,1,0:T(8,128)(2,1)S(1)} %add_convert_fusion.refs_0_), channel_id=1, source_target_pairs={{0,8},{1,9},{2,10},{3,11},{4,12},{5,13},{6,14},{7,15},{8,0},{9,1},... | collective-permute-start | bytes 2359304 | tf_op jit(solution)/shard_map/ppermute | solution.py:609
  342.8 19.7 %collective-permute-start.56 = (bf16[3,256,512]{2,1,0:T(8,128)(2,1)S(1)}, bf16[3,256,512]{2,1,0:T(8,128)(2,1)S(1)}, u32[]{:S(2)}, u32[]{:S(2)}) collective-permute-start(bf16[3,256,512]{2,1,0:T(8,128)(2,1)S(1)} %add_convert_fusion.refs_0_), channel_id=1, source_target_pairs={{0,16},{1,17},{2,18},{3,19},{4,20},{5,21},{6,22},{7,23},{8,24},{9,... | collective-permute-start | bytes 2359304 | tf_op jit(solution)/shard_map/ppermute | solution.py:609
  344.4 60.4 %collective-permute-start.51 = (bf16[512,2048]{1,0:T(8,128)(2,1)}, bf16[512,2048]{1,0:T(8,128)(2,1)}, u32[]{:S(2)}, u32[]{:S(2)}) collective-permute-start(bf16[512,2048]{1,0:T(8,128)(2,1)} %get-tuple-element.255), channel_id=1, source_target_pairs={{0,1},{1,0},{2,3},{3,2},{4,5},{5,4},{6,7},{7,6},{8,9},{9,8},{10,11... | collective-permute-start | bytes 6291464 | tf_op jit(solution)/shard_map/ppermute | solution.py:609
  344.4 18.2 %collective-permute-start.60 = (bf16[3,256,512]{2,1,0:T(8,128)(2,1)S(1)}, bf16[3,256,512]{2,1,0:T(8,128)(2,1)S(1)}, u32[]{:S(2)}, u32[]{:S(2)}) collective-permute-start(bf16[3,256,512]{2,1,0:T(8,128)(2,1)S(1)} %add_convert_fusion.refs_0_), channel_id=1, source_target_pairs={{0,4},{1,5},{2,6},{3,7},{4,0},{5,1},{6,2},{7,3},{8,12},{9,13},{10,... | collective-permute-start | bytes 2359304 | tf_op jit(solution)/shard_map/ppermute | solution.py:609
  344.4 65.5 %collective-permute-start.47 = (bf16[512,2048]{1,0:T(8,128)(2,1)}, bf16[512,2048]{1,0:T(8,128)(2,1)}, u32[]{:S(2)}, u32[]{:S(2)}) collective-permute-start(bf16[512,2048]{1,0:T(8,128)(2,1)} %get-tuple-element.244), channel_id=1, source_target_pairs={{0,4},{1,5},{2,6},{3,7},{4,0},{5,1},{6,2},{7,3},{8,12},{9,13},{10,... | collective-permute-start | bytes 6291464 | tf_op jit(solution)/shard_map/ppermute | solution.py:609
  362.6 19.3 %collective-permute-start.61 = (bf16[3,256,512]{2,1,0:T(8,128)(2,1)S(1)}, bf16[3,256,512]{2,1,0:T(8,128)(2,1)}, u32[]{:S(2)}, u32[]{:S(2)}) collective-permute-start(bf16[3,256,512]{2,1,0:T(8,128)(2,1)S(1)} %collective-permute-done.54.refs_1_), channel_id=1, source_target_pairs={{0,4},{1,5},{2,6},{3,7},{4,0},{5,1},{6,2},{7,3},{8,12},{9,13},{10,... | collective-permute-start | bytes 2359304 | tf_op jit(solution)/shard_map/ppermute | solution.py:609
  363.6 18.8 %collective-permute-start.62 = (bf16[3,256,512]{2,1,0:T(8,128)(2,1)S(1)}, bf16[3,256,512]{2,1,0:T(8,128)(2,1)}, u32[]{:S(2)}, u32[]{:S(2)}) collective-permute-start(bf16[3,256,512]{2,1,0:T(8,128)(2,1)S(1)} %collective-permute-done.56.refs_2_), channel_id=1, source_target_pairs={{0,4},{1,5},{2,6},{3,7},{4,0},{5,1},{6,2},{7,3},{8,12},{9,13},{10,... | collective-permute-start | bytes 2359304 | tf_op jit(solution)/shard_map/ppermute | solution.py:609
  388.6 18.3 %collective-permute-start.63 = (f32[8,512]{1,0:T(8,128)S(1)}, f32[8,512]{1,0:T(8,128)S(1)}, u32[]{:S(2)}, u32[]{:S(2)}) collective-permute-start(f32[8,512]{1,0:T(8,128)S(1)} %copy-done.58), channel_id=1, source_target_pairs={{0,4},{1,5},{2,6},{3,7},{4,0},{5,1},{6,2},{7,3},{8,12},{9,13},{10,... | collective-permute-start | bytes 49160 | tf_op jit(solution)/shard_map/ppermute | solution.py:609
  (98 other events, 980.2 us)
Sparse Core Ops, SparseCore 0:
  16.6 35.9 all-gather.1
